TPU v7x, 256 devices: a whole 4x4x8 slice. The times are simulated.
256 devices in a mesh: crop: 4 (over y), dap: 64 (over x, z, core).
Axes of the slice: x: 4, y: 4, z: 8, core: 2. Of those that a mesh axis runs over, the one named last changes fastest.
Arguments:
- pair: float32 [768, 192, 128], P(('crop', 'dap')), parts along dimension 0, may hold values from -6 to 6
- norm_in: float32 [2, 128], replicated, may hold values from 0.1 to 1.9
- w_proj: bfloat16 [2, 128, 512], replicated, may hold values from -0.5 to 0.5
- w_gate: bfloat16 [2, 128, 128], replicated, may hold values from -0.5 to 0.5
- norm_mid: float32 [2, 128], replicated, may hold values from 0.1 to 1.9
- w_out: bfloat16 [2, 128, 128], replicated, may hold values from -0.5 to 0.5
Outputs:
- pair_out: float32 [768, 192, 128], P(('crop', 'dap')), parts along dimension 0
There are 4 independent parts, one for each index of `crop`. A program takes and returns all parts, laid end to end along the dimension named above; an argument that names none is the same for every part. Nothing has to cross between parts.
All inputs are finite; a program needn't handle non-finite values.
Results may differ from a plain program's by a relative error of at most 0.0049.
Values may be sent and summed in bfloat16 or wider, within the bound.
No kernel may reach another device: no remote copies, remote signals or barrier semaphores. Data moves between devices by JAX's collectives and lax.ppermute only.
A program may use at most 64 MiB of HBM per device.

v0:
```python
import jax
import jax.numpy as jnp
from jax import lax
from jax.sharding import PartitionSpec as P


def layer_norm(value, gain):
    mean = jnp.mean(value, axis=-1, keepdims=True)
    cent = value - mean
    var = jnp.mean(cent * cent, axis=-1, keepdims=True)
    return cent / jnp.sqrt(var + 1e-05) * gain


def project(state, norm_in, w_proj, w_gate, which):
    hidden = w_proj.shape[2] // 4
    normed = layer_norm(state, norm_in[which]).astype(jnp.bfloat16)
    proj = jnp.einsum("ijc,cd->ijd", normed, w_proj[which], preferred_element_type=jnp.float32)
    left = (jax.nn.sigmoid(proj[..., 0:hidden]) * proj[..., hidden : 2 * hidden]).astype(
        jnp.bfloat16
    )
    right = (
        jax.nn.sigmoid(proj[..., 2 * hidden : 3 * hidden]) * proj[..., 3 * hidden : 4 * hidden]
    ).astype(jnp.bfloat16)
    gate = jax.nn.sigmoid(
        jnp.einsum("ijc,cd->ijd", normed, w_gate[which], preferred_element_type=jnp.float32)
    )
    return (left, right, gate)


def finish(state, tri, gate, norm_mid, w_out, which):
    mid = layer_norm(tri, norm_mid[which]).astype(jnp.bfloat16)
    update = jnp.einsum("ijh,hc->ijc", mid, w_out[which], preferred_element_type=jnp.float32)
    return state + gate * update


def per_device(pair, norm_in, w_proj, w_gate, norm_mid, w_out):
    left, right, gate = project(pair, norm_in, w_proj, w_gate, 0)
    tri = jnp.einsum(
        "ikh,jkh->ijh",
        left,
        lax.all_gather(right, "dap", axis=0, tiled=True),
        preferred_element_type=jnp.float32,
    )
    state = finish(pair, tri, gate, norm_mid, w_out, 0)
    left, right, gate = project(state, norm_in, w_proj, w_gate, 1)
    left_cols, right_cols = (
        lax.all_to_all(left, "dap", split_axis=1, concat_axis=0, tiled=True),
        lax.all_to_all(right, "dap", split_axis=1, concat_axis=0, tiled=True),
    )
    tri = jnp.einsum(
        "kih,kjh->ijh",
        left_cols,
        lax.all_gather(right_cols, "dap", axis=1, tiled=True),
        preferred_element_type=jnp.float32,
    )
    return finish(state, tri, gate, norm_mid, w_out, 1)


def solution(mesh):
    return jax.shard_map(
        per_device,
        mesh=mesh,
        in_specs=(P(("crop", "dap"), None, None), P(), P(), P(), P(), P()),
        out_specs=P(("crop", "dap"), None, None),
        check_vma=False,
    )
```

profile of v0, /device:TPU:1, one launch (start us, length us, event | category | flops | bytes accessed | tf_op | source)
XLA Modules:
  0.0 261.7 jit_solution(17711821516486577532)
XLA Ops:
  6.5 1.1 reduce_sum.72
  7.7 1.3 multiply_reduce_fusion.3
  9.0 0.8 slice_bitcast_fusion.1
  9.7 1.4 fusion.28
  11.1 0.8 fusion.16
  12.2 0.8 slice_bitcast_fusion
  13.0 1.3 fusion.7
  14.3 87.0 %all-gather.3.cloned.1.call-done = bf16[192,192,128]{2,1,0:T(8,128)(2,1)} async-done(((bf16[3,192,128]{2,1,0:T(8,128)(2,1)}), bf16[192,192,128]{2,1,0:T(8,128)(2,1)}) %all-gather.3.cloned.1.call-update) | async-done | bytes 9437200 | tf_op jit(solution)/shard_map/all_gather | solution.py:41
  101.3 17.4 %copy.21 = bf16[192,192,128]{1,0,2:T(8,128)(2,1)} copy(bf16[192,192,128]{2,1,0:T(8,128)(2,1)} %all-gather.3.cloned.1.call-done) | data formatting | bytes 18874368 | tf_op jit(solution)/shard_map/all_gather | solution.py:41
  118.7 8.0 %fusion.40 = (f32[3,192]{1,0:T(4,128)S(1)}, f32[3,192,128]{1,0,2:T(4,128)S(1)}) fusion(bf16[192,192,128]{1,0,2:T(8,128)(2,1)} %copy.21, bf16[3,192,128]{1,0,2:T(4,128)(2,1)S(1)} %copy.22), kind=kOutput, calls=%fused_computation.74 | convolution fusion | flops 28384704 | bytes 9881856 | tf_op jit(solution)/shard_map/ikh,jkh->ijh/dot_general | solution.py:38
  127.0 0.2 multiply_convert_fusion.1
  127.2 0.4 fusion.41
  127.6 0.3 multiply_reduce_fusion.2
  127.9 0.4 fusion.26
  128.6 16.6 %all_to_all.36 = bf16[3,192,128]{2,0,1:T(4,128)(2,1)S(1)} all-to-all(bf16[3,192,128]{2,0,1:T(4,128)(2,1)S(1)} %copy.24), channel_id=1, replica_groups=mesh['crop'=4,'dap'=64] {'dap'}, dimensions={1} | all-to-all | bytes 294912 | tf_op jit(solution)/shard_map/all_to_all | solution.py:48
  145.4 0.8 all_to_all.29
  146.1 0.8 copy.27
  147.0 5.7 %all-to-all-start.1 = ((bf16[3,192,128]{2,0,1:T(4,128)(2,1)}), bf16[3,192,128]{2,0,1:T(4,128)(2,1)S(1)}, u32[]{:S(2)}, u32[]{:S(2)}) async-start(bf16[3,192,128]{2,0,1:T(4,128)(2,1)} %copy.27), calls=%async_computation.1 | async-start | bytes 393216 | tf_op jit(solution)/shard_map/all_to_all | solution.py:47
  152.7 0.4 fusion.4
  153.0 10.6 %all-to-all-done.1 = bf16[3,192,128]{2,0,1:T(4,128)(2,1)S(1)} async-done(((bf16[3,192,128]{2,0,1:T(4,128)(2,1)}), bf16[3,192,128]{2,0,1:T(4,128)(2,1)S(1)}, u32[]{:S(2)}, u32[]{:S(2)}) %all-to-all-start.1) | async-done | bytes 147488 | tf_op jit(solution)/shard_map/all_to_all | solution.py:47
  164.0 64.1 %all-gather.5.cloned.1.call-done = bf16[192,192,128]{2,0,1:T(8,128)(2,1)} async-done(((bf16[192,3,128]{2,0,1:T(8,128)(2,1)}), bf16[192,192,128]{2,0,1:T(8,128)(2,1)}) %all-gather.5.cloned.1.call-update) | async-done | bytes 9437200 | tf_op jit(solution)/shard_map/all_gather | solution.py:53
  228.1 17.4 %copy.30 = bf16[192,192,128]{0,1,2:T(8,128)(2,1)} copy(bf16[192,192,128]{2,0,1:T(8,128)(2,1)} %all-gather.5.cloned.1.call-done) | data formatting | bytes 18874368 | tf_op jit(solution)/shard_map/all_gather | solution.py:53
  245.5 7.9 %fusion.42 = (f32[3,192]{1,0:T(4,128)S(1)}, f32[3,192,128]{1,0,2:T(4,128)S(1)}) fusion(bf16[192,192,128]{0,1,2:T(8,128)(2,1)} %copy.30, bf16[192,3,128]{0,1,2:T(4,128)(2,1)S(1)} %copy.31), kind=kOutput, calls=%fused_computation.76 | convolution fusion | flops 28384704 | bytes 9881856 | tf_op jit(solution)/shard_map/kih,kjh->ijh/dot_general | solution.py:50
  253.9 0.9 fusion
  (30 shorter events, 1.7 us)
Async XLA Ops:
  6.5 94.8 %all-gather.3.cloned.1.call-start = ((), (), s32[]{:S(2)}) async-start(), calls=%async_computation.2 | async-start | bytes 9584640 | tf_op jit(solution)/shard_map/all_gather | solution.py:41
  12.0 216.1 %all-gather.5.cloned.1.call-start = ((), (), s32[]{:S(2)}) async-start(), calls=%async_computation.3 | async-start | bytes 9584640 | tf_op jit(solution)/shard_map/all_gather | solution.py:53
  118.7 8.5 %copy-start = (f32[3,192,128]{2,1,0:T(8,128)S(1)}, f32[3,192,128]{2,1,0:T(8,128)}, u32[]{:S(2)}) copy-start(f32[3,192,128]{2,1,0:T(8,128)} %param.6) | copy-start | bytes 884740
  118.7 8.5 %copy-start.2 = (bf16[2,128,128]{2,1,0:T(8,128)(2,1)S(1)}, bf16[2,128,128]{2,1,0:T(8,128)(2,1)}, u32[]{:S(2)}) copy-start(bf16[2,128,128]{2,1,0:T(8,128)(2,1)} %param.11) | copy-start | bytes 196612
  118.7 9.2 %copy-start.1 = (bf16[2,128,512]{2,1,0:T(8,128)(2,1)S(1)}, bf16[2,128,512]{2,1,0:T(8,128)(2,1)}, u32[]{:S(2)}) copy-start(bf16[2,128,512]{2,1,0:T(8,128)(2,1)} %param.8) | copy-start | bytes 786436
  118.7 33.9 %copy-start.3 = (bf16[2,128,128]{2,1,0:T(8,128)(2,1)S(1)}, bf16[2,128,128]{2,1,0:T(8,128)(2,1)}, u32[]{:S(2)}) copy-start(bf16[2,128,128]{2,1,0:T(8,128)(2,1)} %param.9) | copy-start | bytes 196612
  147.0 16.6 %all-to-all-start.1 = ((bf16[3,192,128]{2,0,1:T(4,128)(2,1)}), bf16[3,192,128]{2,0,1:T(4,128)(2,1)S(1)}, u32[]{:S(2)}, u32[]{:S(2)}) async-start(bf16[3,192,128]{2,0,1:T(4,128)(2,1)} %copy.27), calls=%async_computation.1 | async-start | bytes 393216 | tf_op jit(solution)/shard_map/all_to_all | solution.py:47
Sparse Core Ops, SparseCore 0:
  12.1 89.1 all-gather.2
  146.3 81.7 all-gather.4
where the time goes:
time: 263 us; the launch traced here: 262 us
  waiting for transfers between devices  162 us (62%)
  local copies, waits for them, and re-layouts  38.7 us (15%)
  matrix products  20.6 us (8%)
  blocking collectives  16.6 us (6%)
  between operations  13.6 us (5%)
  starting transfers between devices  5.74 us (2%)
  other arithmetic  4.66 us (2%)
    all_gather x1, waiting for transfers between devices, per_device(): lax.all_gather(right, 'dap', axis=0, tiled=True)  87 us
    all_gather x1, waiting for transfers between devices, per_device(): lax.all_gather(right_cols, 'dap', axis=1, tiled=True)  64.1 us
    all_gather x1, local copies, waits for them, and re-layouts, per_device(): lax.all_gather(right, 'dap', axis=0, tiled=True)  17.4 us
    all_gather x1, local copies, waits for them, and re-layouts, per_device(): lax.all_gather(right_cols, 'dap', axis=1, tiled=True)  17.4 us
    all_to_all x1, blocking collectives, per_device(): lax.all_to_all(right, 'dap', split_axis=1, concat_axis=0, tiled=True)  16.6 us
    all_to_all x1, waiting for transfers between devices, per_device(): lax.all_to_all(left, 'dap', split_axis=1, concat_axis=0, tiled=True)  10.6 us
    dot_general x1, matrix products, per_device(): jnp.einsum('ikh,jkh->ijh', left, lax.all_gather(right, 'dap', axis=0, til...  7.98 us
    dot_general x1, matrix products, per_device(): jnp.einsum('kih,kjh->ijh', left_cols, lax.all_gather(right_cols, 'dap', a...  7.91 us
  transfers between devices with their start and end apart: 3, of which 3 were waited for; matrix products, arithmetic and copies ran while one was open for 1% of the time, Pallas kernels for 0%

commit v1 on v0

v1 whole, which is shorter than its diff:
```python
import jax
import jax.numpy as jnp
from jax import lax
from jax.sharding import PartitionSpec as P


def layer_norm(value, gain, axis):
    mean = jnp.mean(value, axis=axis, keepdims=True)
    cent = value - mean
    var = jnp.mean(cent * cent, axis=axis, keepdims=True)
    return cent / jnp.sqrt(var + 1e-05) * gain


def per_device(pair, norm_in, w_proj, w_gate, norm_mid, w_out):
    rows, cols, chans = pair.shape
    hidden = w_proj.shape[2] // 4
    parts = cols // rows
    own = hidden // parts

    def project(state, which):
        normed = layer_norm(state, norm_in[which], -1).astype(jnp.bfloat16)
        proj = jnp.einsum(
            "cd,ijc->dij", w_proj[which], normed, preferred_element_type=jnp.float32
        ).reshape(4, hidden, rows, cols)
        left = (jax.nn.sigmoid(proj[0]) * proj[1]).astype(jnp.bfloat16)
        right = (jax.nn.sigmoid(proj[2]) * proj[3]).astype(jnp.bfloat16)
        gate = jax.nn.sigmoid(
            jnp.einsum("ijc,cd->ijd", normed, w_gate[which], preferred_element_type=jnp.float32)
        )
        both = jnp.stack(
            [left.reshape(parts, own, rows, cols), right.reshape(parts, own, rows, cols)], axis=1
        )
        return both.reshape(parts, 2 * own, rows * cols), gate

    def to_channels(both):
        got = lax.all_to_all(both, "dap", 0, 0, tiled=True)
        got = got.reshape(parts, 2, own, rows, cols).transpose(1, 2, 0, 3, 4)
        got = got.reshape(2, own, cols, cols)
        return got[0], got[1]

    def to_rows(tri):
        send = tri.astype(jnp.bfloat16).reshape(own, parts, rows, cols).transpose(1, 0, 2, 3)
        got = lax.all_to_all(send.reshape(parts, own * rows, cols), "dap", 0, 0, tiled=True)
        return got.reshape(hidden, rows, cols).astype(jnp.float32)

    def finish(state, tri, gate, which):
        mid = layer_norm(tri, norm_mid[which][:, None, None], 0).astype(jnp.bfloat16)
        update = jnp.einsum("hij,hc->ijc", mid, w_out[which], preferred_element_type=jnp.float32)
        return state + gate * update

    both, gate = project(pair, 0)
    left, right = to_channels(both)
    tri = jnp.einsum("hik,hjk->hij", left, right, preferred_element_type=jnp.float32)
    state = finish(pair, to_rows(tri), gate, 0)
    both, gate = project(state, 1)
    left, right = to_channels(both)
    tri = jnp.einsum("hki,hkj->hij", left, right, preferred_element_type=jnp.float32)
    return finish(state, to_rows(tri), gate, 1)


def solution(mesh):
    return jax.shard_map(
        per_device,
        mesh=mesh,
        in_specs=(P(("crop", "dap"), None, None), P(), P(), P(), P(), P()),
        out_specs=P(("crop", "dap"), None, None),
        check_vma=False,
    )
```

time: 263 us -> 101 us (0.38)
  waiting for transfers between devices: 162 us -> 22.6 us
  blocking collectives: 16.6 us -> 45.1 us
  local copies, waits for them, and re-layouts: 38.7 us -> 10.5 us
  matrix products: 20.6 us -> 4.28 us
  between operations: 13.6 us -> 0.48 us
  starting transfers between devices: 5.74 us -> 12.3 us
    all_gather x2 -> x0, waiting for transfers between devices: 151 us -> none  [the longest x1 87 us: per_device(): lax.all_gather(right, 'dap', axis=0, tiled=True)]
    all_gather x2 -> x0, local copies, waits for them, and re-layouts: 34.8 us -> none  [the longest x1 17.4 us: per_device(): lax.all_gather(right, 'dap', axis=0, tiled=True)]
    all_to_all x1 -> x2, blocking collectives: 16.6 us -> 45.1 us  [to_channels(): got = lax.all_to_all(both, 'dap', 0, 0, tiled=True)]
    dot_general x6, matrix products: 19 us -> 3.56 us  [the longest x2 1.75 us: project(): jnp.einsum('cd,ijc->dij', w_proj[which], normed, preferred_element_type=j...]
    all_to_all x1 -> x2, waiting for transfers between devices: 10.6 us -> 22.6 us  [to_rows(): lax.all_to_all(send.reshape(parts, own * rows, cols), 'dap', 0, 0, tiled=...]
    all_to_all x1 -> x2, starting transfers between devices: 5.7 us -> 12.3 us  [to_rows(): lax.all_to_all(send.reshape(parts, own * rows, cols), 'dap', 0, 0, tiled=...]
    reshape x0 -> x8, local copies, waits for them, and re-layouts: none -> 4.03 us  [the longest x4 1.96 us: project(): return (both.reshape(parts, 2 * own, rows * cols), gate)]
  transfers between devices with their start and end apart: 3 -> 2, of which waited for: 3 -> 2; matrix products, arithmetic and copies ran while one was open for 1% -> 1% of each run, Pallas kernels for 0% -> 0%
where the time goes in v1:
time: 101 us
  blocking collectives  45.1 us (45%)
  waiting for transfers between devices  22.6 us (22%)
  starting transfers between devices  12.3 us (12%)
  local copies, waits for them, and re-layouts  10.5 us (10%)
  other arithmetic  5.38 us (5%)
  matrix products  4.28 us (4%)
    all_to_all x2, blocking collectives, to_channels(): got = lax.all_to_all(both, 'dap', 0, 0, tiled=True)  45.1 us
    all_to_all x2, waiting for transfers between devices, to_rows(): lax.all_to_all(send.reshape(parts, own * rows, cols), 'dap', 0, 0, tiled=...  22.6 us
    all_to_all x2, starting transfers between devices, to_rows(): lax.all_to_all(send.reshape(parts, own * rows, cols), 'dap', 0, 0, tiled=...  12.3 us
  transfers between devices with their start and end apart: 2, of which 2 were waited for; matrix products, arithmetic and copies ran while one was open for 1% of the time, Pallas kernels for 0%

profile of v1, /device:TPU:1, one launch (start us, length us, event | category | flops | bytes accessed | tf_op | source)
XLA Modules:
  0.0 100.7 jit_solution(11367515340879923888)
XLA Ops:
  0.0 1.1 %reduce_sum.72 = f32[3,192]{1,0:T(4,128)S(1)} reduce(f32[3,192,128]{2,1,0:T(8,128)} %param.6, f32[]{:T(128)} %constant.16.clone.1), dimensions={2}, to_apply=%region_0.0 | reduce | flops 73152 | bytes 297220 | tf_op jit(solution)/shard_map/reduce_sum | solution.py:8
  1.2 1.3 %multiply_reduce_fusion.3 = f32[3,192]{1,0:T(4,128)S(1)} fusion(f32[3,192,128]{2,1,0:T(8,128)} %param.6, f32[3,192]{1,0:T(4,128)S(1)} %broadcast_multiply_fusion.3), kind=kLoop, calls=%fused_computation.49 | loop fusion | flops 220608 | bytes 299520 | tf_op jit(solution)/shard_map/reduce_sum | solution.py:10
  2.4 0.8 slice_bitcast_fusion
  3.2 1.4 %convolution_bitcast_fusion.1 = f32[512,3,192]{0,2,1:T(8,128)S(1)} fusion(bf16[2,128,512]{2,1,0:T(8,128)(2,1)} %param.8, f32[3,192,128]{2,1,0:T(8,128)} %param.6, f32[128]{0:T(128)S(1)} %get-tuple-element.16, f32[3,192]{1,0:T(4,128)S(1)} %add_sqrt_fusion.3, f32[3,192]{1,0:T(4,128)S(1)} %broadcast_multiply_fusion.3), kind=kOutput, calls=%fused_computation.1 | convolution fusion | flops 75792384 | bytes 1610752 | tf_op jit(solution)/shard_map/cd,ijc->dij/dot_general | solution.py:22
  5.3 0.6 pad_maximum_fusion
  5.9 0.5 copy.68
  6.5 0.4 reshape.300
  6.9 26.0 %all_to_all.20 = bf16[64,4,576]{2,1,0:T(4,128)(2,1)S(1)} all-to-all(bf16[64,4,576]{2,1,0:T(4,128)(2,1)S(1)} %reshape.300), channel_id=1, replica_groups=mesh['crop'=4,'dap'=64] {'dap'}, dimensions={0} | all-to-all | bytes 589824 | tf_op jit(solution)/shard_map/all_to_all | solution.py:36
  34.4 0.8 copy.49
  35.2 6.2 %all-to-all-start.1 = ((bf16[64,6,192]{2,1,0:T(8,128)(2,1)}), bf16[64,6,192]{2,1,0:T(8,128)(2,1)S(1)}, u32[]{:S(2)}, u32[]{:S(2)}) async-start(bf16[64,6,192]{2,1,0:T(8,128)(2,1)} %copy.49), calls=%async_computation.1 | async-start | bytes 524288 | tf_op jit(solution)/shard_map/all_to_all | solution.py:43
  41.8 0.4 fusion.7
  42.1 11.3 %all-to-all-done.1 = bf16[64,6,192]{2,1,0:T(8,128)(2,1)S(1)} async-done(((bf16[64,6,192]{2,1,0:T(8,128)(2,1)}), bf16[64,6,192]{2,1,0:T(8,128)(2,1)S(1)}, u32[]{:S(2)}, u32[]{:S(2)}) %all-to-all-start.1) | async-done | bytes 147488 | tf_op jit(solution)/shard_map/all_to_all | solution.py:43
  54.8 0.5 copy-done.2
  55.4 0.4 fusion.44
  56.1 0.4 convolution_bitcast_fusion
  57.2 0.6 pad_maximum_fusion.1
  57.8 0.5 copy.69
  58.4 0.4 reshape.301
  58.8 19.1 %all_to_all.21 = bf16[64,4,576]{2,1,0:T(4,128)(2,1)S(1)} all-to-all(bf16[64,4,576]{2,1,0:T(4,128)(2,1)S(1)} %reshape.301), channel_id=1, replica_groups=mesh['crop'=4,'dap'=64] {'dap'}, dimensions={0} | all-to-all | bytes 589824 | tf_op jit(solution)/shard_map/all_to_all | solution.py:36
  79.3 0.8 copy.64
  80.1 6.2 %all-to-all-start.3 = ((bf16[64,6,192]{2,1,0:T(8,128)(2,1)}), bf16[64,6,192]{2,1,0:T(8,128)(2,1)S(1)}, u32[]{:S(2)}, u32[]{:S(2)}) async-start(bf16[64,6,192]{2,1,0:T(8,128)(2,1)} %copy.64), calls=%async_computation.3 | async-start | bytes 524288 | tf_op jit(solution)/shard_map/all_to_all | solution.py:43
  86.6 0.4 fusion.4
  87.0 11.3 %all-to-all-done.3 = bf16[64,6,192]{2,1,0:T(8,128)(2,1)S(1)} async-done(((bf16[64,6,192]{2,1,0:T(8,128)(2,1)}), bf16[64,6,192]{2,1,0:T(8,128)(2,1)S(1)}, u32[]{:S(2)}, u32[]{:S(2)}) %all-to-all-start.3) | async-done | bytes 147488 | tf_op jit(solution)/shard_map/all_to_all | solution.py:43
  99.7 0.9 fusion
  (73 shorter events, 7.9 us)
Async XLA Ops:
  33.9 7.5 %copy-start.3 = (f32[2,128]{1,0:T(2,128)S(1)}, f32[2,128]{1,0:T(2,128)}, u32[]{:S(2)}) copy-start(f32[2,128]{1,0:T(2,128)} %param.10) | copy-start | bytes 3076
  33.9 7.9 %copy-start = (f32[3,192,128]{2,1,0:T(8,128)S(1)}, f32[3,192,128]{2,1,0:T(8,128)}, u32[]{:S(2)}) copy-start(f32[3,192,128]{2,1,0:T(8,128)} %param.6) | copy-start | bytes 884740
  33.9 7.9 %copy-start.4 = (bf16[2,128,128]{2,1,0:T(8,128)(2,1)S(1)}, bf16[2,128,128]{2,1,0:T(8,128)(2,1)}, u32[]{:S(2)}) copy-start(bf16[2,128,128]{2,1,0:T(8,128)(2,1)} %param.9) | copy-start | bytes 196612
  35.2 18.2 %all-to-all-start.1 = ((bf16[64,6,192]{2,1,0:T(8,128)(2,1)}), bf16[64,6,192]{2,1,0:T(8,128)(2,1)S(1)}, u32[]{:S(2)}, u32[]{:S(2)}) async-start(bf16[64,6,192]{2,1,0:T(8,128)(2,1)} %copy.49), calls=%async_computation.1 | async-start | bytes 524288 | tf_op jit(solution)/shard_map/all_to_all | solution.py:43
  54.5 0.8 copy-start.2
  54.7 1.4 %copy-start.1 = (bf16[2,128,512]{2,1,0:T(8,128)(2,1)S(1)}, bf16[2,128,512]{2,1,0:T(8,128)(2,1)}, u32[]{:S(2)}) copy-start(bf16[2,128,512]{2,1,0:T(8,128)(2,1)} %param.8) | copy-start | bytes 786436
  80.1 18.2 %all-to-all-start.3 = ((bf16[64,6,192]{2,1,0:T(8,128)(2,1)}), bf16[64,6,192]{2,1,0:T(8,128)(2,1)S(1)}, u32[]{:S(2)}, u32[]{:S(2)}) async-start(bf16[64,6,192]{2,1,0:T(8,128)(2,1)} %copy.64), calls=%async_computation.3 | async-start | bytes 524288 | tf_op jit(solution)/shard_map/all_to_all | solution.py:43

commit v2 on v1

v2 whole, which is shorter than its diff:
```python
import jax
import jax.numpy as jnp
from jax import lax
from jax.experimental import pallas as pl
from jax.experimental.pallas import tpu as pltpu
from jax.sharding import PartitionSpec as P

F32 = jnp.float32
BF16 = jnp.bfloat16
LANES = 128


def column(row):
    return jnp.transpose(jnp.broadcast_to(row, (8, row.shape[1])))[:, 0:1]


def norm_rows(value, gain):
    mean = jnp.mean(value, axis=0, keepdims=True)
    cent = value - mean
    var = jnp.mean(cent * cent, axis=0, keepdims=True)
    return (cent * lax.rsqrt(var + 1e-05) * gain).astype(BF16)


def mix(weight, value):
    return lax.dot_general(weight, value, (((0,), (0,)), ((), ())), preferred_element_type=F32)


def project(state, gain, w_proj, w_gate, both, gate):
    hidden = w_gate.shape[0]
    half = hidden // 2
    normed = norm_rows(state, gain)
    for side in range(2):
        proj = mix(w_proj[:, 2 * side * hidden : 2 * (side + 1) * hidden], normed)
        edge = (jax.nn.sigmoid(proj[:hidden]) * proj[hidden:]).astype(BF16)
        both[2 * side] = edge[:half]
        both[2 * side + 1] = edge[half:]
    gate[...] = jax.nn.sigmoid(mix(w_gate, normed))


def first_kernel(pair, norm_in, w_proj, w_gate, both, gate, state):
    rows, cols, chans = pair.shape
    value = jnp.transpose(pair[...].reshape(rows * cols, chans))
    state[...] = value
    project(value, column(norm_in[0:1, :]), w_proj[0], w_gate[0], both, gate)


def finished(got, state, gate, norm_mid, w_out):
    tri = got[...].astype(F32).reshape(state.shape)
    return state[...] + gate[...] * mix(w_out, norm_rows(tri, norm_mid))


def middle_kernel(
    got, state, gate, norm_in, w_proj, w_gate, norm_mid, w_out, both, gate_next, state_next
):
    value = finished(got, state, gate, column(norm_mid[0:1, :]), w_out[0])
    state_next[...] = value
    project(value, column(norm_in[1:2, :]), w_proj[0], w_gate[0], both, gate_next)


def last_kernel(got, state, gate, norm_mid, w_out, out):
    value = finished(got, state, gate, column(norm_mid[1:2, :]), w_out[0])
    out[...] = jnp.transpose(value).reshape(out.shape)


def stacked(value, cols):
    return jnp.concatenate([value[:, k : k + cols] for k in range(0, value.shape[1], cols)], axis=0)


def outgoing_kernel(got, out, scratch):
    parts, places = got.shape[1:]
    cols = scratch.shape[1]
    rows = cols // parts
    rest = cols - LANES
    for chan in range(2):
        right = jnp.concatenate(
            [got[2 + chan].astype(F32), jnp.zeros((parts, LANES - rest), F32)], axis=1
        )
        for k in range(rows):
            for piece in range(2):
                start = k * cols + piece * LANES
                scratch[piece, pl.ds(k, parts, stride=rows), :] = right[:, start : start + LANES]
        folded = jnp.concatenate([scratch[0], scratch[1][:, :rest]], axis=1).astype(BF16)
        tri = lax.dot_general(
            stacked(got[chan], cols),
            folded,
            (((1,), (1,)), ((), ())),
            preferred_element_type=F32,
        ).astype(BF16)
        for k in range(rows):
            out[chan, :, k * cols : (k + 1) * cols] = tri[k * parts : (k + 1) * parts]


def incoming_kernel(got, out, scratch):
    parts = got.shape[1]
    cols = scratch.shape[1]
    rows = cols // parts
    rest = cols - LANES
    for chan in range(2):
        tri = mix(stacked(got[chan], cols), stacked(got[2 + chan], cols))
        scratch[0] = tri[:, :LANES]
        scratch[1] = jnp.concatenate([tri[:, LANES:], jnp.zeros((cols, LANES - rest), F32)], axis=1)
        for k in range(rows):
            picked = [scratch[piece, pl.ds(k, parts, stride=rows), :] for piece in range(2)]
            out[chan, :, k * cols : (k + 1) * cols] = jnp.concatenate(
                [picked[0], picked[1][:, :rest]], axis=1
            ).astype(BF16)


def per_device(pair, norm_in, w_proj, w_gate, norm_mid, w_out):
    rows, cols, chans = pair.shape
    hidden = w_proj.shape[2] // 4
    parts = cols // rows
    places = rows * cols
    both_t = jax.ShapeDtypeStruct((4, parts, places), BF16)
    tri_t = jax.ShapeDtypeStruct((2, parts, places), BF16)
    flat_t = jax.ShapeDtypeStruct((chans, places), F32)
    params = pltpu.CompilerParams(vmem_limit_bytes=32 * 2**20)

    def whole(shape):
        return pl.BlockSpec(shape, lambda i: (0,) * len(shape))

    def chosen(array, which):
        return pl.BlockSpec((1,) + array.shape[1:], lambda i: (which, 0, 0))

    def call(kernel, ins, in_specs, outs, scratch=()):
        return pl.pallas_call(
            kernel,
            grid=(1,),
            in_specs=in_specs,
            out_specs=[whole(o.shape) for o in outs],
            out_shape=outs,
            scratch_shapes=scratch,
            compiler_params=params,
        )(*ins)

    def exchange(value):
        return lax.all_to_all(value, "dap", 1, 1, tiled=True)

    square = [pltpu.VMEM((2, cols, LANES), F32)]
    both, gate, state = call(
        first_kernel,
        (pair, norm_in, w_proj, w_gate),
        [whole(pair.shape), whole(norm_in.shape), chosen(w_proj, 0), chosen(w_gate, 0)],
        [both_t, flat_t, flat_t],
    )
    (tri,) = call(outgoing_kernel, (exchange(both),), [whole(both_t.shape)], [tri_t], square)
    both, gate, state = call(
        middle_kernel,
        (exchange(tri), state, gate, norm_in, w_proj, w_gate, norm_mid, w_out),
        [
            whole(tri_t.shape),
            whole(flat_t.shape),
            whole(flat_t.shape),
            whole(norm_in.shape),
            chosen(w_proj, 1),
            chosen(w_gate, 1),
            whole(norm_mid.shape),
            chosen(w_out, 0),
        ],
        [both_t, flat_t, flat_t],
    )
    (tri,) = call(incoming_kernel, (exchange(both),), [whole(both_t.shape)], [tri_t], square)
    (out,) = call(
        last_kernel,
        (exchange(tri), state, gate, norm_mid, w_out),
        [
            whole(tri_t.shape),
            whole(flat_t.shape),
            whole(flat_t.shape),
            whole(norm_mid.shape),
            chosen(w_out, 1),
        ],
        [jax.ShapeDtypeStruct(pair.shape, F32)],
    )
    return out


def solution(mesh):
    return jax.shard_map(
        per_device,
        mesh=mesh,
        in_specs=(P(("crop", "dap"), None, None), P(), P(), P(), P(), P()),
        out_specs=P(("crop", "dap"), None, None),
        check_vma=False,
    )
```

time: 101 us -> 86.8 us (0.86)
  blocking collectives: 45.1 us -> 77.7 us
  waiting for transfers between devices: 22.6 us -> 0 us
  starting transfers between devices: 12.3 us -> 0 us
  other arithmetic: 5.38 us -> 0 us
  local copies, waits for them, and re-layouts: 10.5 us -> 5.21 us
  matrix products: 4.28 us -> 0 us
  Pallas kernels: 0 us -> 3.45 us
    all_to_all x2 -> x4, blocking collectives: 45.1 us -> 77.7 us  [exchange(): return lax.all_to_all(value, 'dap', 1, 1, tiled=True)]
    all_to_all x2 -> x0, waiting for transfers between devices: 22.6 us -> none  [to_rows(): lax.all_to_all(send.reshape(parts, own * rows, cols), 'dap', 0, 0, tiled=...]
    all_to_all x2 -> x0, starting transfers between devices: 12.3 us -> none  [to_rows(): lax.all_to_all(send.reshape(parts, own * rows, cols), 'dap', 0, 0, tiled=...]
    dot_general x8 -> x0, matrix products: 4.28 us -> none  [the longest x2 1.75 us: project(): jnp.einsum('cd,ijc->dij', w_proj[which], normed, preferred_element_type=j...]
    reshape x8 -> x0, local copies, waits for them, and re-layouts: 4.03 us -> none  [the longest x4 1.96 us: project(): return (both.reshape(parts, 2 * own, rows * cols), gate)]
    unnamed x10 -> x16, local copies, waits for them, and re-layouts: 0.56 us -> 4.24 us
    pallas_call x0 -> x5, Pallas kernels: none -> 3.45 us  [call(): pl.pallas_call(kernel, grid=(1,), in_specs=in_specs, out_specs=[whole(o.s...]
    reduce_sum x7 -> x0, other arithmetic: 3.43 us -> none  [the longest x4 1.98 us: layer_norm(): var = jnp.mean(cent * cent, axis=axis, keepdims=True)]
  transfers between devices with their start and end apart: 2 -> 0, of which waited for: 2 -> 0; matrix products, arithmetic and copies ran while one was open for 1% -> 0% of each run, Pallas kernels for 0% -> 0%
where the time goes in v2:
time: 86.8 us; the launch traced here: 86.4 us
  blocking collectives  77.7 us (90%)
  local copies, waits for them, and re-layouts  5.21 us (6%)
  Pallas kernels  3.45 us (4%)
    all_to_all x4, blocking collectives, exchange(): return lax.all_to_all(value, 'dap', 1, 1, tiled=True)  77.7 us
    unnamed x16, local copies, waits for them, and re-layouts  4.24 us
    pallas_call x5, Pallas kernels, call(): pl.pallas_call(kernel, grid=(1,), in_specs=in_specs, out_specs=[whole(o.s...  3.45 us

profile of v2, /device:TPU:1, one launch (start us, length us, event | category | flops | bytes accessed | tf_op | source)
XLA Modules:
  0.0 86.4 jit_solution(12497809970950405913)
XLA Ops:
  0.0 0.0 copy-start
  0.0 0.9 %copy-done = bf16[2,128,512]{2,1,0:T(8,128)(2,1)S(1)} copy-done((bf16[2,128,512]{2,1,0:T(8,128)(2,1)S(1)}, bf16[2,128,512]{2,1,0:T(8,128)(2,1)}, u32[]{:S(2)}) %copy-start) | copy-done | bytes 262168
  1.0 1.0 %copy-done.2 = f32[3,192,128]{2,1,0:T(8,128)S(1)} copy-done((f32[3,192,128]{2,1,0:T(8,128)S(1)}, f32[3,192,128]{2,1,0:T(8,128)}, u32[]{:S(2)}) %copy-start.2) | copy-done | bytes 294936
  1.9 0.8 copy-done.3
  2.8 0.7 copy-done.5
  3.4 0.7 shard_map.64
  4.1 0.3 copy.7
  4.4 26.0 %all_to_all.20 = bf16[4,64,576]{2,0,1:T(4,128)(2,1)S(1)} all-to-all(bf16[4,64,576]{2,0,1:T(4,128)(2,1)S(1)} %copy.7), channel_id=1, replica_groups=mesh['crop'=4,'dap'=64] {'dap'}, dimensions={1} | all-to-all | bytes 589824 | tf_op jit(solution)/shard_map/all_to_all | solution.py:137
  30.5 0.4 shard_map.65
  30.8 0.2 copy.9
  31.0 0.0 copy-start.1
  31.0 16.7 %all_to_all.21 = bf16[2,64,576]{2,0,1:T(2,128)(2,1)S(1)} all-to-all(bf16[2,64,576]{2,0,1:T(2,128)(2,1)S(1)} %copy.9), channel_id=1, replica_groups=mesh['crop'=4,'dap'=64] {'dap'}, dimensions={1} | all-to-all | bytes 294912 | tf_op jit(solution)/shard_map/all_to_all | solution.py:137
  47.8 0.0 copy-start.6
  47.8 0.0 copy-done.1
  47.8 0.8 copy-done.4
  48.6 0.0 copy-done.7
  48.6 0.0 copy-done.6
  48.6 0.8 shard_map.66
  49.4 0.3 copy.11
  49.7 18.4 %all_to_all.22 = bf16[4,64,576]{2,0,1:T(4,128)(2,1)S(1)} all-to-all(bf16[4,64,576]{2,0,1:T(4,128)(2,1)S(1)} %copy.11), channel_id=1, replica_groups=mesh['crop'=4,'dap'=64] {'dap'}, dimensions={1} | all-to-all | bytes 589824 | tf_op jit(solution)/shard_map/all_to_all | solution.py:137
  68.1 0.4 shard_map.67
  68.5 0.2 copy.13
  68.7 16.6 %all_to_all.23 = bf16[2,64,576]{2,0,1:T(2,128)(2,1)S(1)} all-to-all(bf16[2,64,576]{2,0,1:T(2,128)(2,1)S(1)} %copy.13), channel_id=1, replica_groups=mesh['crop'=4,'dap'=64] {'dap'}, dimensions={1} | all-to-all | bytes 294912 | tf_op jit(solution)/shard_map/all_to_all | solution.py:137
  85.3 1.2 %shard_map.68 = f32[3,192,128]{2,1,0:T(8,128)} custom-call(bf16[2,64,576]{2,1,0:T(8,128)(2,1)S(1)} %copy.14.got, f32[128,576]{1,0:T(8,128)S(1)} %get-tuple-element.15.state, f32[128,576]{1,0:T(8,128)S(1)} %get-tuple-element.16.gate, f32[2,128]{1,0:T(2,128)S(1)} %copy-done.7, bf16[2,128,128]{2,1,0:T(8,128)(2,1)S(1)} %copy-done.4), custom_call_target="tpu_custom_call" | custom-call | tf_op jit(solution)/shard_map/pallas_call | solution.py:126
  (9 shorter events, 0.1 us)
Async XLA Ops:
  0.0 0.9 %copy-start = (bf16[2,128,512]{2,1,0:T(8,128)(2,1)S(1)}, bf16[2,128,512]{2,1,0:T(8,128)(2,1)}, u32[]{:S(2)}) copy-start(bf16[2,128,512]{2,1,0:T(8,128)(2,1)} %w_proj.3) | copy-start | bytes 786436
  1.0 1.0 %copy-start.2 = (f32[3,192,128]{2,1,0:T(8,128)S(1)}, f32[3,192,128]{2,1,0:T(8,128)}, u32[]{:S(2)}) copy-start(f32[3,192,128]{2,1,0:T(8,128)} %pair.1) | copy-start | bytes 884740
  1.9 0.8 copy-start.3
  2.8 0.7 copy-start.5
  31.0 16.7 %copy-start.1 = (bf16[2,128,512]{2,1,0:T(8,128)(2,1)S(1)}, bf16[2,128,512]{2,1,0:T(8,128)(2,1)}, u32[]{:S(2)}) copy-start(bf16[2,128,512]{2,1,0:T(8,128)(2,1)} %w_proj.3) | copy-start | bytes 786436
  47.7 0.8 copy-start.4
  47.7 0.8 copy-start.7
  47.8 0.8 copy-start.6

commit v3 on v2

v3 whole, which is shorter than its diff:
```python
import jax
import jax.numpy as jnp
from jax import lax
from jax.experimental import pallas as pl
from jax.experimental.pallas import tpu as pltpu
from jax.sharding import PartitionSpec as P

F32 = jnp.float32
BF16 = jnp.bfloat16
LANES = 128


def column(row):
    return jnp.transpose(jnp.broadcast_to(row, (8, row.shape[1])))[:, 0:1]


def norm_rows(value, gain):
    mean = jnp.mean(value, axis=0, keepdims=True)
    cent = value - mean
    var = jnp.mean(cent * cent, axis=0, keepdims=True)
    return (cent * lax.rsqrt(var + 1e-05) * gain).astype(BF16)


def mix(weight, value):
    return lax.dot_general(weight, value, (((0,), (0,)), ((), ())), preferred_element_type=F32)


def project(state, gain, w_proj, both):
    hidden = w_proj.shape[1] // 4
    half = hidden // 2
    normed = norm_rows(state, gain)
    for side in range(2):
        proj = mix(w_proj[:, 2 * side * hidden : 2 * (side + 1) * hidden], normed)
        edge = (jax.nn.sigmoid(proj[:hidden]) * proj[hidden:]).astype(BF16)
        both[side] = jnp.concatenate([edge[:half], edge[half:]], axis=1)
    return normed


def first_kernel(
    pair,
    norm_in,
    w_proj,
    w_gate,
    norm_mid,
    w_out,
    both,
    gate,
    state,
    norm_in_near,
    w_proj_near,
    w_gate_near,
    norm_mid_near,
    w_out_near,
    pair_near,
    sems,
):
    rows, cols, chans = pair.shape
    moves = [
        pltpu.make_async_copy(far, near, sems.at[k])
        for k, (far, near) in enumerate(
            [
                (pair, pair_near),
                (norm_in, norm_in_near),
                (w_proj, w_proj_near),
                (w_gate, w_gate_near),
                (norm_mid, norm_mid_near),
                (w_out, w_out_near),
            ]
        )
    ]
    for move in moves:
        move.start()
    for move in moves[:3]:
        move.wait()
    value = jnp.transpose(pair_near[...].reshape(rows * cols, chans))
    state[...] = value
    normed = project(value, column(norm_in_near[0:1, :]), w_proj_near[0], both)
    moves[3].wait()
    gate[...] = jax.nn.sigmoid(mix(w_gate_near[0], normed))
    for move in moves[4:]:
        move.wait()


def middle_kernel(
    got, state, gate, norm_in, w_proj, w_gate, norm_mid, w_out, both, gate_next, state_next
):
    tri = got[...].astype(F32).reshape(state.shape)
    mid = norm_rows(tri, column(norm_mid[0:1, :]))
    value = state[...] + gate[...] * mix(w_out[0], mid)
    state_next[...] = value
    normed = project(value, column(norm_in[1:2, :]), w_proj[1], both)
    gate_next[...] = jax.nn.sigmoid(mix(w_gate[1], normed))


def last_kernel(got, state, gate, norm_mid, w_out, out, near, sems):
    rows, cols, chans = out.shape
    gain = column(norm_mid[1:2, :])
    moves = []
    for k in range(rows):
        part = slice(k * cols, (k + 1) * cols)
        tri = got[:, :, part].astype(F32).reshape(chans, cols)
        value = state[:, part] + gate[:, part] * mix(w_out[1], norm_rows(tri, gain))
        near[k] = jnp.transpose(value)
        move = pltpu.make_async_copy(near.at[k], out.at[k], sems.at[k])
        move.start()
        moves.append(move)
    for move in moves:
        move.wait()


def stacked(value, cols):
    return jnp.concatenate([value[:, k : k + cols] for k in range(0, value.shape[1], cols)], axis=0)


def outgoing_kernel(got, out, scratch):
    chans, parts, places = out.shape
    cols = scratch.shape[1]
    rows = cols // parts
    rest = cols - LANES
    for chan in range(chans):
        part = slice(chan * places, (chan + 1) * places)
        right = jnp.concatenate(
            [got[1, :, part].astype(F32), jnp.zeros((parts, LANES - rest), F32)], axis=1
        )
        for k in range(rows):
            for piece in range(2):
                start = k * cols + piece * LANES
                scratch[piece, pl.ds(k, parts, stride=rows), :] = right[:, start : start + LANES]
        folded = jnp.concatenate([scratch[0], scratch[1][:, :rest]], axis=1).astype(BF16)
        tri = lax.dot_general(
            stacked(got[0, :, part], cols),
            folded,
            (((1,), (1,)), ((), ())),
            preferred_element_type=F32,
        ).astype(BF16)
        for k in range(rows):
            out[chan, :, k * cols : (k + 1) * cols] = tri[k * parts : (k + 1) * parts]


def incoming_kernel(got, out, scratch):
    chans, parts, places = out.shape
    cols = scratch.shape[1]
    rows = cols // parts
    rest = cols - LANES
    for chan in range(chans):
        part = slice(chan * places, (chan + 1) * places)
        tri = mix(stacked(got[0, :, part], cols), stacked(got[1, :, part], cols))
        scratch[0] = tri[:, :LANES]
        scratch[1] = jnp.concatenate([tri[:, LANES:], jnp.zeros((cols, LANES - rest), F32)], axis=1)
        for k in range(rows):
            picked = [scratch[piece, pl.ds(k, parts, stride=rows), :] for piece in range(2)]
            out[chan, :, k * cols : (k + 1) * cols] = jnp.concatenate(
                [picked[0], picked[1][:, :rest]], axis=1
            ).astype(BF16)


def per_device(pair, norm_in, w_proj, w_gate, norm_mid, w_out):
    rows, cols, chans = pair.shape
    parts = cols // rows
    places = rows * cols
    both_t = jax.ShapeDtypeStruct((2, parts, 2 * places), BF16)
    tri_t = jax.ShapeDtypeStruct((2, parts, places), BF16)
    flat_t = jax.ShapeDtypeStruct((chans, places), F32)
    near = pl.BlockSpec(memory_space=pltpu.VMEM)
    far = pl.BlockSpec(memory_space=pl.ANY)
    dma = pltpu.SemaphoreType.DMA

    def call(kernel, ins, outs, scratch=(), in_spec=near, out_spec=near):
        return pl.pallas_call(
            kernel,
            in_specs=[in_spec] * len(ins),
            out_specs=[out_spec] * len(outs),
            out_shape=outs,
            scratch_shapes=scratch,
            compiler_params=pltpu.CompilerParams(vmem_limit_bytes=32 * 2**20),
        )(*ins)

    def exchange(value):
        return lax.all_to_all(value, "dap", 1, 1, tiled=True)

    def like(array):
        return jax.ShapeDtypeStruct(array.shape, array.dtype)

    square = [pltpu.VMEM((2, cols, LANES), F32)]
    params = (norm_in, w_proj, w_gate, norm_mid, w_out)
    both, gate, state, *params = call(
        first_kernel,
        tuple(pltpu.with_memory_space_constraint(a, pltpu.HBM) for a in (pair, *params)),
        [both_t, flat_t, flat_t, *map(like, params)],
        [pltpu.VMEM(pair.shape, F32), dma((6,))],
        in_spec=far,
    )
    norm_mid, w_out = params[3:]
    (tri,) = call(outgoing_kernel, (exchange(both),), [tri_t], square)
    both, gate, state = call(
        middle_kernel, (exchange(tri), state, gate, *params), [both_t, flat_t, flat_t]
    )
    (tri,) = call(incoming_kernel, (exchange(both),), [tri_t], square)
    (out,) = call(
        last_kernel,
        (exchange(tri), state, gate, norm_mid, w_out),
        [like(pair)],
        [pltpu.VMEM(pair.shape, F32), dma((rows,))],
        out_spec=far,
    )
    return out


def solution(mesh):
    return jax.shard_map(
        per_device,
        mesh=mesh,
        in_specs=(P(("crop", "dap"), None, None), P(), P(), P(), P(), P()),
        out_specs=P(("crop", "dap"), None, None),
        check_vma=False,
    )
```

time: 86.8 us -> 82.8 us (0.954)
  local copies, waits for them, and re-layouts: 5.21 us -> 1.06 us
  Pallas kernels: 3.45 us -> 5.24 us
  blocking collectives: 77.7 us -> 76.2 us
    unnamed x16 -> x0, local copies, waits for them, and re-layouts: 4.24 us -> none
    pallas_call x5, Pallas kernels: 3.45 us -> 5.24 us  [call(): pl.pallas_call(kernel, in_specs=[in_spec] * len(ins), out_specs=[out_spec...]
    all_to_all x4, blocking collectives: 77.7 us -> 76.2 us  [exchange(): return lax.all_to_all(value, 'dap', 1, 1, tiled=True)]
where the time goes in v3:
time: 82.8 us; the launch traced here: 82.5 us
  blocking collectives  76.2 us (92%)
  Pallas kernels  5.24 us (6%)
  local copies, waits for them, and re-layouts  1.06 us (1%)
    all_to_all x4, blocking collectives, exchange(): return lax.all_to_all(value, 'dap', 1, 1, tiled=True)  76.2 us
    pallas_call x5, Pallas kernels, call(): pl.pallas_call(kernel, in_specs=[in_spec] * len(ins), out_specs=[out_spec...  5.24 us

profile of v3, /device:TPU:1, one launch (start us, length us, event | category | flops | bytes accessed | tf_op | source)
XLA Modules:
  0.0 82.5 jit_solution(10159864760354702973)
XLA Ops:
  0.0 2.1 %shard_map.64 = (bf16[2,64,1152]{2,1,0:T(8,128)(2,1)S(1)}, f32[128,576]{1,0:T(8,128)S(1)}, f32[128,576]{1,0:T(8,128)S(1)}, f32[2,128]{1,0:T(2,128)S(1)}, bf16[2,...) custom-call(f32[3,192,128]{2,1,0:T(8,128)} %pair.1, ...), custom_call_target="tpu_custom_call" | custom-call | tf_op jit(solution)/shard_map/pallas_call | solution.py:169
  2.1 0.3 copy.7
  2.4 25.4 %all_to_all.20 = bf16[2,64,1152]{2,0,1:T(2,128)(2,1)S(1)} all-to-all(bf16[2,64,1152]{2,0,1:T(2,128)(2,1)S(1)} %copy.7), channel_id=1, replica_groups=mesh['crop'=4,'dap'=64] {'dap'}, dimensions={1} | all-to-all | bytes 589824 | tf_op jit(solution)/shard_map/all_to_all | solution.py:179
  27.9 0.5 shard_map.65
  28.4 0.2 copy.9
  28.5 16.5 %all_to_all.21 = bf16[2,64,576]{2,0,1:T(2,128)(2,1)S(1)} all-to-all(bf16[2,64,576]{2,0,1:T(2,128)(2,1)S(1)} %copy.9), channel_id=1, replica_groups=mesh['crop'=4,'dap'=64] {'dap'}, dimensions={1} | all-to-all | bytes 294912 | tf_op jit(solution)/shard_map/all_to_all | solution.py:179
  45.0 0.8 %shard_map.66 = (bf16[2,64,1152]{2,1,0:T(8,128)(2,1)S(1)}, f32[128,576]{1,0:T(8,128)S(1)}, f32[128,576]{1,0:T(8,128)S(1)}) custom-call(bf16[2,64,576]{2,1,0:T(8,128)(2,1)S(1)} %copy.10.got, f32[128,576]{1,0:T(8,128)S(1)} %get-tuple-element.17.state, f32[128,576]{1,0:T(8,128)S(1)} %get-tuple-element.18.gate, f32[2,128]{1,0:T(2,128)S(1)} %get-tuple-element.19.norm_in, ...), custom_call_target="tpu_custom_call" | custom-call | tf_op jit(solution)/shard_map/pallas_call | solution.py:169
  45.9 0.3 copy.11
  46.2 17.8 %all_to_all.22 = bf16[2,64,1152]{2,0,1:T(2,128)(2,1)S(1)} all-to-all(bf16[2,64,1152]{2,0,1:T(2,128)(2,1)S(1)} %copy.11), channel_id=1, replica_groups=mesh['crop'=4,'dap'=64] {'dap'}, dimensions={1} | all-to-all | bytes 589824 | tf_op jit(solution)/shard_map/all_to_all | solution.py:179
  64.0 0.5 shard_map.67
  64.5 0.2 copy.13
  64.7 16.5 %all_to_all.23 = bf16[2,64,576]{2,0,1:T(2,128)(2,1)S(1)} all-to-all(bf16[2,64,576]{2,0,1:T(2,128)(2,1)S(1)} %copy.13), channel_id=1, replica_groups=mesh['crop'=4,'dap'=64] {'dap'}, dimensions={1} | all-to-all | bytes 294912 | tf_op jit(solution)/shard_map/all_to_all | solution.py:179
  81.1 1.4 %shard_map.68 = f32[3,192,128]{2,1,0:T(8,128)} custom-call(bf16[2,64,576]{2,1,0:T(8,128)(2,1)S(1)} %copy.14.got, f32[128,576]{1,0:T(8,128)S(1)} %get-tuple-element.25.state, f32[128,576]{1,0:T(8,128)S(1)} %get-tuple-element.26.gate, f32[2,128]{1,0:T(2,128)S(1)} %get-tuple-element.22.norm_mid, bf16[2,128,128]{2,1,0:T(8,128)(2,1)S(1)} %get-tuple-element.23.w_out), custom_call_target="tpu_custom_call" | custom-call | tf_op jit(solution)/shard_map/pallas_call | solution.py:169
  (4 shorter events, 0.1 us)

commit v4 on v3

v4 whole, which is shorter than its diff:
```python
import math

import jax
import jax.numpy as jnp
from jax import lax
from jax.experimental import pallas as pl
from jax.experimental.pallas import tpu as pltpu
from jax.sharding import PartitionSpec as P

F32 = jnp.float32
BF16 = jnp.bfloat16


def column(row):
    return jnp.transpose(jnp.broadcast_to(row, (8, row.shape[1])))[:, 0:1]


def norm_rows(value, gain):
    mean = jnp.mean(value, axis=0, keepdims=True)
    cent = value - mean
    var = jnp.mean(cent * cent, axis=0, keepdims=True)
    return (cent * lax.rsqrt(var + 1e-05) * gain).astype(BF16)


def mix(weight, value):
    return lax.dot_general(weight, value, (((0,), (0,)), ((), ())), preferred_element_type=F32)


def sigmoid(value):
    return 0.5 * jnp.tanh(0.5 * value) + 0.5


def project(state, gain, w_proj, both):
    hidden = w_proj.shape[1] // 4
    half = hidden // 2
    normed = norm_rows(state, gain)
    for side in range(2):
        proj = mix(w_proj[:, 2 * side * hidden : 2 * (side + 1) * hidden], normed)
        edge = (sigmoid(proj[:hidden]) * proj[hidden:]).astype(BF16)
        both[side] = jnp.concatenate([edge[:half], edge[half:]], axis=1)
    return normed


def first_kernel(
    pair,
    norm_in,
    w_proj,
    w_gate,
    norm_mid,
    w_out,
    both,
    gate,
    state,
    norm_in_near,
    w_proj_near,
    w_gate_near,
    norm_mid_near,
    w_out_near,
    pair_near,
    sems,
):
    rows, cols, chans = pair.shape
    half = cols // 2
    pairs = [
        (norm_in, norm_in_near),
        *((pair.at[k, pl.ds(h, half)], pair_near.at[k, pl.ds(h, half)]) for k in range(rows) for h in (0, half)),
        (w_proj.at[0], w_proj_near.at[0]),
        (w_gate, w_gate_near),
        (w_proj.at[1], w_proj_near.at[1]),
        (norm_mid, norm_mid_near),
        (w_out, w_out_near),
    ]
    moves = [pltpu.make_async_copy(*ends, sems.at[k]) for k, ends in enumerate(pairs)]
    for move in moves:
        move.start()
    for move in moves[:7]:
        move.wait()
    parts = cols // rows
    value = jnp.transpose(
        jnp.concatenate(
            [
                pair_near[k, pl.ds(j, parts, stride=rows), :]
                for k in range(rows)
                for j in range(rows)
            ],
            axis=0,
        )
    )
    state[...] = value
    gain = column(norm_in_near[0:1, :])
    moves[7].wait()
    normed = project(value, gain, w_proj_near[0], both)
    moves[8].wait()
    gate[...] = sigmoid(mix(w_gate_near[0], normed))
    for move in moves[9:]:
        move.wait()


def middle_kernel(
    got, state, gate, norm_in, w_proj, w_gate, norm_mid, w_out, both, gate_next, state_next
):
    tri = got[...].astype(F32).reshape(state.shape)
    mid = norm_rows(tri, column(norm_mid[0:1, :]))
    value = state[...] + gate[...] * mix(w_out[0], mid)
    state_next[...] = value
    normed = project(value, column(norm_in[1:2, :]), w_proj[1], both)
    gate_next[...] = sigmoid(mix(w_gate[1], normed))


def last_kernel(got, state, gate, norm_mid, w_out, out, near, sems):
    rows, cols, chans = out.shape
    parts = cols // rows
    gain = column(norm_mid[1:2, :])
    moves = []
    for k, stop in ((0, rows - 1), (rows - 1, rows)):
        part = slice(k * cols, stop * cols)
        tri = got[:, :, part].astype(F32).reshape(chans, -1)
        value = state[:, part] + gate[:, part] * mix(w_out[1], norm_rows(tri, gain))
        block = pl.ds(k, stop - k)
        turned = jnp.transpose(value)
        for piece in range((stop - k) * rows):
            near[k + piece // rows, pl.ds(piece % rows, parts, stride=rows), :] = turned[
                piece * parts : (piece + 1) * parts
            ]
        move = pltpu.make_async_copy(near.at[block], out.at[block], sems.at[len(moves)])
        move.start()
        moves.append(move)
    for move in moves:
        move.wait()


def stacked(value, cols):
    return jnp.concatenate([value[:, k : k + cols] for k in range(0, value.shape[1], cols)], axis=0)


def product(got, out, dims):
    chans, parts, places = out.shape
    cols = math.isqrt(parts * places)
    for chan in range(chans):
        part = slice(chan * places, (chan + 1) * places)
        left, right = (stacked(got[side, :, part], cols) for side in range(2))
        tri = lax.dot_general(left, right, (dims, ((), ())), preferred_element_type=F32)
        tri = tri.astype(BF16)
        out[chan] = jnp.concatenate([tri[k : k + parts] for k in range(0, cols, parts)], axis=1)


def outgoing_kernel(got, out):
    product(got, out, ((1,), (1,)))


def incoming_kernel(got, out):
    product(got, out, ((0,), (0,)))


def per_device(pair, norm_in, w_proj, w_gate, norm_mid, w_out):
    rows, cols, chans = pair.shape
    parts = cols // rows
    places = rows * cols
    both_t = jax.ShapeDtypeStruct((2, parts, 2 * places), BF16)
    tri_t = jax.ShapeDtypeStruct((2, parts, places), BF16)
    flat_t = jax.ShapeDtypeStruct((chans, places), F32)
    near = pl.BlockSpec(memory_space=pltpu.VMEM)
    far = pl.BlockSpec(memory_space=pl.ANY)
    dma = pltpu.SemaphoreType.DMA

    def call(kernel, ins, outs, scratch=(), in_spec=near, out_spec=near):
        return pl.pallas_call(
            kernel,
            in_specs=[in_spec] * len(ins),
            out_specs=[out_spec] * len(outs),
            out_shape=outs,
            scratch_shapes=scratch,
            compiler_params=pltpu.CompilerParams(vmem_limit_bytes=32 * 2**20),
        )(*ins)

    def exchange(value):
        return lax.all_to_all(value, "dap", 1, 1, tiled=True)

    def like(array):
        return jax.ShapeDtypeStruct(array.shape, array.dtype)

    params = (norm_in, w_proj, w_gate, norm_mid, w_out)
    both, gate, state, *params = call(
        first_kernel,
        tuple(pltpu.with_memory_space_constraint(a, pltpu.HBM) for a in (pair, *params)),
        [both_t, flat_t, flat_t, *map(like, params)],
        [pltpu.VMEM(pair.shape, F32), dma((12,))],
        in_spec=far,
    )
    norm_mid, w_out = params[3:]
    (tri,) = call(outgoing_kernel, (exchange(both),), [tri_t])
    both, gate, state = call(
        middle_kernel, (exchange(tri), state, gate, *params), [both_t, flat_t, flat_t]
    )
    (tri,) = call(incoming_kernel, (exchange(both),), [tri_t])
    (out,) = call(
        last_kernel,
        (exchange(tri), state, gate, norm_mid, w_out),
        [like(pair)],
        [pltpu.VMEM(pair.shape, F32), dma((2,))],
        out_spec=far,
    )
    return out


def solution(mesh):
    return jax.shard_map(
        per_device,
        mesh=mesh,
        in_specs=(P(("crop", "dap"), None, None), P(), P(), P(), P(), P()),
        out_specs=P(("crop", "dap"), None, None),
        check_vma=False,
    )
```

time: 82.8 us -> 82.3 us (level)
  no operation moved by 1% of the time
where the time goes in v4:
time: 82.3 us; the launch traced here: 82.1 us
  blocking collectives  76.2 us (93%)
  Pallas kernels  4.81 us (6%)
  local copies, waits for them, and re-layouts  1.06 us (1%)
    all_to_all x4, blocking collectives, exchange(): return lax.all_to_all(value, 'dap', 1, 1, tiled=True)  76.2 us
    pallas_call x5, Pallas kernels, call(): pl.pallas_call(kernel, in_specs=[in_spec] * len(ins), out_specs=[out_spec...  4.81 us

profile of v4, /device:TPU:1, one launch (start us, length us, event | category | flops | bytes accessed | tf_op | source)
XLA Modules:
  0.0 82.1 jit_solution(650254028558260348)
XLA Ops:
  0.0 1.9 %shard_map.64 = (bf16[2,64,1152]{2,1,0:T(8,128)(2,1)S(1)}, f32[128,576]{1,0:T(8,128)S(1)}, f32[128,576]{1,0:T(8,128)S(1)}, f32[2,128]{1,0:T(2,128)S(1)}, bf16[2,...) custom-call(f32[3,192,128]{2,1,0:T(8,128)} %pair.1, ...), custom_call_target="tpu_custom_call" | custom-call | tf_op jit(solution)/shard_map/pallas_call | solution.py:167
  1.9 0.3 copy.7
  2.3 25.4 %all_to_all.20 = bf16[2,64,1152]{2,0,1:T(2,128)(2,1)S(1)} all-to-all(bf16[2,64,1152]{2,0,1:T(2,128)(2,1)S(1)} %copy.7), channel_id=1, replica_groups=mesh['crop'=4,'dap'=64] {'dap'}, dimensions={1} | all-to-all | bytes 589824 | tf_op jit(solution)/shard_map/all_to_all | solution.py:177
  27.7 0.4 shard_map.65
  28.2 0.2 copy.9
  28.3 16.5 %all_to_all.21 = bf16[2,64,576]{2,0,1:T(2,128)(2,1)S(1)} all-to-all(bf16[2,64,576]{2,0,1:T(2,128)(2,1)S(1)} %copy.9), channel_id=1, replica_groups=mesh['crop'=4,'dap'=64] {'dap'}, dimensions={1} | all-to-all | bytes 294912 | tf_op jit(solution)/shard_map/all_to_all | solution.py:177
  44.8 0.8 %shard_map.66 = (bf16[2,64,1152]{2,1,0:T(8,128)(2,1)S(1)}, f32[128,576]{1,0:T(8,128)S(1)}, f32[128,576]{1,0:T(8,128)S(1)}) custom-call(bf16[2,64,576]{2,1,0:T(8,128)(2,1)S(1)} %copy.10.got, f32[128,576]{1,0:T(8,128)S(1)} %get-tuple-element.17.state, f32[128,576]{1,0:T(8,128)S(1)} %get-tuple-element.18.gate, f32[2,128]{1,0:T(2,128)S(1)} %get-tuple-element.19.norm_in, ...), custom_call_target="tpu_custom_call" | custom-call | tf_op jit(solution)/shard_map/pallas_call | solution.py:167
  45.7 0.3 copy.11
  46.0 17.8 %all_to_all.22 = bf16[2,64,1152]{2,0,1:T(2,128)(2,1)S(1)} all-to-all(bf16[2,64,1152]{2,0,1:T(2,128)(2,1)S(1)} %copy.11), channel_id=1, replica_groups=mesh['crop'=4,'dap'=64] {'dap'}, dimensions={1} | all-to-all | bytes 589824 | tf_op jit(solution)/shard_map/all_to_all | solution.py:177
  63.8 0.4 shard_map.67
  64.2 0.2 copy.13
  64.4 16.5 %all_to_all.23 = bf16[2,64,576]{2,0,1:T(2,128)(2,1)S(1)} all-to-all(bf16[2,64,576]{2,0,1:T(2,128)(2,1)S(1)} %copy.13), channel_id=1, replica_groups=mesh['crop'=4,'dap'=64] {'dap'}, dimensions={1} | all-to-all | bytes 294912 | tf_op jit(solution)/shard_map/all_to_all | solution.py:177
  80.9 1.2 %shard_map.68 = f32[3,192,128]{2,1,0:T(8,128)} custom-call(bf16[2,64,576]{2,1,0:T(8,128)(2,1)S(1)} %copy.14.got, f32[128,576]{1,0:T(8,128)S(1)} %get-tuple-element.25.state, f32[128,576]{1,0:T(8,128)S(1)} %get-tuple-element.26.gate, f32[2,128]{1,0:T(2,128)S(1)} %get-tuple-element.22.norm_mid, bf16[2,128,128]{2,1,0:T(8,128)(2,1)S(1)} %get-tuple-element.23.w_out), custom_call_target="tpu_custom_call" | custom-call | tf_op jit(solution)/shard_map/pallas_call | solution.py:167
  (4 shorter events, 0.1 us)

commit v5 on v4

--- a/solution.py
+++ b/solution.py
@@ -9,6 +9,7 @@
 
 F32 = jnp.float32
 BF16 = jnp.bfloat16
+SCALE = 2.0**-6
 
 
 def column(row):
@@ -99,7 +100,7 @@
 def middle_kernel(
     got, state, gate, norm_in, w_proj, w_gate, norm_mid, w_out, both, gate_next, state_next
 ):
-    tri = got[...].astype(F32).reshape(state.shape)
+    tri = got[...].reshape(state.shape)
     mid = norm_rows(tri, column(norm_mid[0:1, :]))
     value = state[...] + gate[...] * mix(w_out[0], mid)
     state_next[...] = value
@@ -114,7 +115,7 @@
     moves = []
     for k, stop in ((0, rows - 1), (rows - 1, rows)):
         part = slice(k * cols, stop * cols)
-        tri = got[:, :, part].astype(F32).reshape(chans, -1)
+        tri = got[:, :, part].reshape(chans, -1)
         value = state[:, part] + gate[:, part] * mix(w_out[1], norm_rows(tri, gain))
         block = pl.ds(k, stop - k)
         turned = jnp.transpose(value)
@@ -140,7 +141,6 @@
         part = slice(chan * places, (chan + 1) * places)
         left, right = (stacked(got[side, :, part], cols) for side in range(2))
         tri = lax.dot_general(left, right, (dims, ((), ())), preferred_element_type=F32)
-        tri = tri.astype(BF16)
         out[chan] = jnp.concatenate([tri[k : k + parts] for k in range(0, cols, parts)], axis=1)
 
 
@@ -157,7 +157,7 @@
     parts = cols // rows
     places = rows * cols
     both_t = jax.ShapeDtypeStruct((2, parts, 2 * places), BF16)
-    tri_t = jax.ShapeDtypeStruct((2, parts, places), BF16)
+    tri_t = jax.ShapeDtypeStruct((2, parts, places), F32)
     flat_t = jax.ShapeDtypeStruct((chans, places), F32)
     near = pl.BlockSpec(memory_space=pltpu.VMEM)
     far = pl.BlockSpec(memory_space=pl.ANY)
@@ -176,6 +176,10 @@
     def exchange(value):
         return lax.all_to_all(value, "dap", 1, 1, tiled=True)
 
+    def exchange_half(value):
+        value = exchange((value * SCALE).astype(jnp.float16))
+        return value.astype(F32) * (1 / SCALE)
+
     def like(array):
         return jax.ShapeDtypeStruct(array.shape, array.dtype)
 
@@ -190,12 +194,12 @@
     norm_mid, w_out = params[3:]
     (tri,) = call(outgoing_kernel, (exchange(both),), [tri_t])
     both, gate, state = call(
-        middle_kernel, (exchange(tri), state, gate, *params), [both_t, flat_t, flat_t]
+        middle_kernel, (exchange_half(tri), state, gate, *params), [both_t, flat_t, flat_t]
     )
     (tri,) = call(incoming_kernel, (exchange(both),), [tri_t])
     (out,) = call(
         last_kernel,
-        (exchange(tri), state, gate, norm_mid, w_out),
+        (exchange_half(tri), state, gate, norm_mid, w_out),
         [like(pair)],
         [pltpu.VMEM(pair.shape, F32), dma((2,))],
         out_spec=far,

time: 82.3 us -> 82.5 us (level)
  no operation moved by 1% of the time
where the time goes in v5:
time: 82.5 us; the launch traced here: 82.3 us
  blocking collectives  76.2 us (92%)
  Pallas kernels  4.78 us (6%)
  local copies, waits for them, and re-layouts  1.11 us (1%)
    all_to_all x4, blocking collectives, exchange(): return lax.all_to_all(value, 'dap', 1, 1, tiled=True)  76.2 us
    pallas_call x5, Pallas kernels, call(): pl.pallas_call(kernel, in_specs=[in_spec] * len(ins), out_specs=[out_spec...  4.78 us

profile of v5, /device:TPU:1, one launch (start us, length us, event | category | flops | bytes accessed | tf_op | source)
XLA Modules:
  0.0 82.3 jit_solution(15029262217685164574)
XLA Ops:
  0.0 1.9 %shard_map.64 = (bf16[2,64,1152]{2,1,0:T(8,128)(2,1)S(1)}, f32[128,576]{1,0:T(8,128)S(1)}, f32[128,576]{1,0:T(8,128)S(1)}, f32[2,128]{1,0:T(2,128)S(1)}, bf16[2,...) custom-call(f32[3,192,128]{2,1,0:T(8,128)} %pair.1, ...), custom_call_target="tpu_custom_call" | custom-call | tf_op jit(solution)/shard_map/pallas_call | solution.py:167
  1.9 0.3 copy.7
  2.3 25.4 %all_to_all.20 = bf16[2,64,1152]{2,0,1:T(2,128)(2,1)S(1)} all-to-all(bf16[2,64,1152]{2,0,1:T(2,128)(2,1)S(1)} %copy.7), channel_id=1, replica_groups=mesh['crop'=4,'dap'=64] {'dap'}, dimensions={1} | all-to-all | bytes 589824 | tf_op jit(solution)/shard_map/all_to_all | solution.py:177
  27.7 0.4 shard_map.65
  28.2 0.2 copy.9
  28.4 16.5 %all_to_all.21 = f16[2,64,576]{2,0,1:T(2,128)(2,1)S(1)} all-to-all(f16[2,64,576]{2,0,1:T(2,128)(2,1)S(1)} %copy.9), channel_id=1, replica_groups=mesh['crop'=4,'dap'=64] {'dap'}, dimensions={1} | all-to-all | bytes 294912 | tf_op jit(solution)/shard_map/all_to_all | solution.py:177
  45.0 0.8 shard_map.66
  45.8 0.3 copy.11
  46.1 17.8 %all_to_all.22 = bf16[2,64,1152]{2,0,1:T(2,128)(2,1)S(1)} all-to-all(bf16[2,64,1152]{2,0,1:T(2,128)(2,1)S(1)} %copy.11), channel_id=1, replica_groups=mesh['crop'=4,'dap'=64] {'dap'}, dimensions={1} | all-to-all | bytes 589824 | tf_op jit(solution)/shard_map/all_to_all | solution.py:177
  63.9 0.4 shard_map.67
  64.4 0.2 copy.13
  64.6 16.5 %all_to_all.23 = f16[2,64,576]{2,0,1:T(2,128)(2,1)S(1)} all-to-all(f16[2,64,576]{2,0,1:T(2,128)(2,1)S(1)} %copy.13), channel_id=1, replica_groups=mesh['crop'=4,'dap'=64] {'dap'}, dimensions={1} | all-to-all | bytes 294912 | tf_op jit(solution)/shard_map/all_to_all | solution.py:177
  81.1 1.2 %shard_map.68 = f32[3,192,128]{2,1,0:T(8,128)} custom-call(f32[2,64,576]{2,1,0:T(8,128)S(1)} %convert_multiply_fusion.got, f32[128,576]{1,0:T(8,128)S(1)} %get-tuple-element.25.state, f32[128,576]{1,0:T(8,128)S(1)} %get-tuple-element.26.gate, f32[2,128]{1,0:T(2,128)S(1)} %get-tuple-element.22.norm_mid, bf16[2,128,128]{2,1,0:T(8,128)(2,1)S(1)} %get-tuple-element.23.w_out), custom_call_target="tpu_custom_call" | custom-call | tf_op jit(solution)/shard_map/pallas_call | solution.py:167
  (6 shorter events, 0.2 us)

commit v6 on v4

--- a/solution.py
+++ b/solution.py
@@ -9,6 +9,8 @@
 
 F32 = jnp.float32
 BF16 = jnp.bfloat16
+SCALE = 2.0**-6
+LANES = 128
 
 
 def column(row):
@@ -30,15 +32,9 @@
     return 0.5 * jnp.tanh(0.5 * value) + 0.5
 
 
-def project(state, gain, w_proj, both):
-    hidden = w_proj.shape[1] // 4
-    half = hidden // 2
-    normed = norm_rows(state, gain)
-    for side in range(2):
-        proj = mix(w_proj[:, 2 * side * hidden : 2 * (side + 1) * hidden], normed)
-        edge = (sigmoid(proj[:hidden]) * proj[hidden:]).astype(BF16)
-        both[side] = jnp.concatenate([edge[:half], edge[half:]], axis=1)
-    return normed
+def edge(proj):
+    hidden = proj.shape[0] // 2
+    return (sigmoid(proj[:hidden]) * proj[hidden:]).astype(BF16)
 
 
 def first_kernel(
@@ -89,32 +85,41 @@
     state[...] = value
     gain = column(norm_in_near[0:1, :])
     moves[7].wait()
-    normed = project(value, gain, w_proj_near[0], both)
     moves[8].wait()
-    gate[...] = sigmoid(mix(w_gate_near[0], normed))
+    normed = norm_rows(value, gain)
+    weights = jnp.concatenate([w_proj_near[0], w_gate_near[0]], axis=1)
+    proj = mix(weights, normed)
+    both[...] = jnp.concatenate(
+        [edge(proj[: 2 * chans]), edge(proj[2 * chans : 4 * chans])], axis=1
+    )
+    gate[...] = sigmoid(proj[4 * chans :])
     for move in moves[9:]:
         move.wait()
 
 
 def middle_kernel(
-    got, state, gate, norm_in, w_proj, w_gate, norm_mid, w_out, both, gate_next, state_next
+    got, state, gate, norm_in, w_proj, w_gate, gains, w_out, both, gate_next, state_next
 ):
-    tri = got[...].astype(F32).reshape(state.shape)
-    mid = norm_rows(tri, column(norm_mid[0:1, :]))
+    tri = got[...]
+    mid = norm_rows(tri, gains[0][:, 0:1])
     value = state[...] + gate[...] * mix(w_out[0], mid)
     state_next[...] = value
-    normed = project(value, column(norm_in[1:2, :]), w_proj[1], both)
+    normed = norm_rows(value, column(norm_in[1:2, :]))
+    wide = w_proj.shape[2] // 2
+    both[...] = jnp.concatenate(
+        [edge(mix(w_proj[1][:, :wide], normed)), edge(mix(w_proj[1][:, wide:], normed))], axis=1
+    )
     gate_next[...] = sigmoid(mix(w_gate[1], normed))
 
 
-def last_kernel(got, state, gate, norm_mid, w_out, out, near, sems):
+def last_kernel(got, state, gate, gains, w_out, out, near, sems):
     rows, cols, chans = out.shape
     parts = cols // rows
-    gain = column(norm_mid[1:2, :])
+    gain = gains[1][:, 0:1]
     moves = []
     for k, stop in ((0, rows - 1), (rows - 1, rows)):
         part = slice(k * cols, stop * cols)
-        tri = got[:, :, part].astype(F32).reshape(chans, -1)
+        tri = got[:, part]
         value = state[:, part] + gate[:, part] * mix(w_out[1], norm_rows(tri, gain))
         block = pl.ds(k, stop - k)
         turned = jnp.transpose(value)
@@ -133,31 +138,48 @@
     return jnp.concatenate([value[:, k : k + cols] for k in range(0, value.shape[1], cols)], axis=0)
 
 
-def product(got, out, dims):
-    chans, parts, places = out.shape
+def product(got, out, scratch, dims):
+    chans, parts, lanes = got.shape
+    places = lanes // 2
     cols = math.isqrt(parts * places)
+    spare = jnp.zeros((parts, scratch.shape[0] * LANES - places), F32)
     for chan in range(chans):
-        part = slice(chan * places, (chan + 1) * places)
-        left, right = (stacked(got[side, :, part], cols) for side in range(2))
+        left, right = (
+            stacked(got[chan, :, side * places : (side + 1) * places], cols) for side in range(2)
+        )
         tri = lax.dot_general(left, right, (dims, ((), ())), preferred_element_type=F32)
-        tri = tri.astype(BF16)
-        out[chan] = jnp.concatenate([tri[k : k + parts] for k in range(0, cols, parts)], axis=1)
-
-
-def outgoing_kernel(got, out):
-    product(got, out, ((1,), (1,)))
-
-
-def incoming_kernel(got, out):
-    product(got, out, ((0,), (0,)))
+        tri = [tri[k : k + parts] for k in range(0, cols, parts)]
+        tri = jnp.concatenate([*tri, spare], axis=1)
+        for k in range(scratch.shape[0]):
+            scratch[k, pl.ds(chan, parts, stride=chans), :] = tri[:, k * LANES : (k + 1) * LANES]
+    tri = jnp.concatenate([scratch[k] for k in range(scratch.shape[0])], axis=1)
+    out[...] = tri[:, :places]
+
+
+def outgoing_kernel(got, norm_mid, w_out, out, gains, w_out_turned, tiles, scratch):
+    product(got, out, tiles, ((1,), (1,)))
+    half = scratch.shape[0] // 2
+    for which in range(2):
+        gain = jnp.broadcast_to(norm_mid[which : which + 1, :], scratch.shape)
+        for value, turned in ((jnp.transpose(gain), gains), (w_out[which].astype(F32), w_out_turned)):
+            scratch[...] = value
+            for slot in range(2):
+                turned[which, slot * half : (slot + 1) * half] = scratch[
+                    pl.ds(slot, half, stride=2), :
+                ].astype(turned.dtype)
+
+
+def incoming_kernel(got, out, tiles):
+    product(got, out, tiles, ((0,), (0,)))
 
 
 def per_device(pair, norm_in, w_proj, w_gate, norm_mid, w_out):
     rows, cols, chans = pair.shape
     parts = cols // rows
     places = rows * cols
-    both_t = jax.ShapeDtypeStruct((2, parts, 2 * places), BF16)
-    tri_t = jax.ShapeDtypeStruct((2, parts, places), BF16)
+    both_t = jax.ShapeDtypeStruct((chans, 2 * places), BF16)
+    tri_t = jax.ShapeDtypeStruct((chans, places), F32)
+    tiles = pltpu.VMEM((pl.cdiv(places, LANES), chans, LANES), F32)
     flat_t = jax.ShapeDtypeStruct((chans, places), F32)
     near = pl.BlockSpec(memory_space=pltpu.VMEM)
     far = pl.BlockSpec(memory_space=pl.ANY)
@@ -173,8 +195,15 @@
             compiler_params=pltpu.CompilerParams(vmem_limit_bytes=32 * 2**20),
         )(*ins)
 
-    def exchange(value):
-        return lax.all_to_all(value, "dap", 1, 1, tiled=True)
+    def to_channels(both):
+        both = both.reshape(parts, 2, 2 * places)
+        return jnp.swapaxes(lax.all_to_all(both, "dap", 0, 0, tiled=True), 0, 1)
+
+    def to_rows(tri):
+        tri = (tri * SCALE).astype(jnp.float16).reshape(parts, 2, places)
+        tri = jnp.swapaxes(lax.all_to_all(tri, "dap", 0, 0, tiled=True), 0, 1)
+        tri = lax.optimization_barrier(tri)
+        return tri.astype(F32).reshape(chans, places) * (1 / SCALE)
 
     def like(array):
         return jax.ShapeDtypeStruct(array.shape, array.dtype)
@@ -187,15 +216,19 @@
         [pltpu.VMEM(pair.shape, F32), dma((12,))],
         in_spec=far,
     )
-    norm_mid, w_out = params[3:]
-    (tri,) = call(outgoing_kernel, (exchange(both),), [tri_t])
+    tri, gains, w_out = call(
+        outgoing_kernel,
+        (to_channels(both), *params[3:]),
+        [tri_t, jax.ShapeDtypeStruct(w_out.shape, F32), like(w_out)],
+        [tiles, pltpu.VMEM(w_out.shape[1:], F32)],
+    )
     both, gate, state = call(
-        middle_kernel, (exchange(tri), state, gate, *params), [both_t, flat_t, flat_t]
-    )
-    (tri,) = call(incoming_kernel, (exchange(both),), [tri_t])
+        middle_kernel, (to_rows(tri), state, gate, *params[:3], gains, w_out), [both_t, flat_t, flat_t]
+    )
+    (tri,) = call(incoming_kernel, (to_channels(both),), [tri_t], [tiles])
     (out,) = call(
         last_kernel,
-        (exchange(tri), state, gate, norm_mid, w_out),
+        (to_rows(tri), state, gate, gains, w_out),
         [like(pair)],
         [pltpu.VMEM(pair.shape, F32), dma((2,))],
         out_spec=far,

time: 82.3 us -> 81.6 us (level)
    pallas_call x4 -> x0, local copies, waits for them, and re-layouts: 0.95 us -> none  [call(): pl.pallas_call(kernel, in_specs=[in_spec] * len(ins), out_specs=[out_spec...]
where the time goes in v6:
time: 81.6 us; the launch traced here: 81.4 us
  blocking collectives  76.2 us (93%)
  Pallas kernels  4.41 us (5%)
    all_to_all x2, blocking collectives, to_channels(): return jnp.swapaxes(lax.all_to_all(both, 'dap', 0, 0, tiled=True), 0, 1)  43.2 us
    all_to_all x2, blocking collectives, to_rows(): tri = jnp.swapaxes(lax.all_to_all(tri, 'dap', 0, 0, tiled=True), 0, 1)  32.9 us
    pallas_call x5, Pallas kernels, call(): pl.pallas_call(kernel, in_specs=[in_spec] * len(ins), out_specs=[out_spec...  4.41 us

profile of v6, /device:TPU:1, one launch (start us, length us, event | category | flops | bytes accessed | tf_op | source)
XLA Modules:
  0.0 81.4 jit_solution(12524225288169543651)
XLA Ops:
  0.0 1.7 %shard_map.64 = (bf16[128,1152]{1,0:T(8,128)(2,1)S(1)}, f32[128,576]{1,0:T(8,128)S(1)}, f32[128,576]{1,0:T(8,128)S(1)}, f32[2,128]{1,0:T(2,128)S(1)}, bf16[2,128...) custom-call(f32[3,192,128]{2,1,0:T(8,128)} %pair.1, ...), custom_call_target="tpu_custom_call" | custom-call | tf_op jit(solution)/shard_map/pallas_call | solution.py:189
  1.7 0.1 reshape.18
  1.8 25.4 %all_to_all.20 = bf16[64,2,1152]{2,1,0:T(2,128)(2,1)S(1)} all-to-all(bf16[64,2,1152]{2,1,0:T(2,128)(2,1)S(1)} %reshape.18), channel_id=1, replica_groups=mesh['crop'=4,'dap'=64] {'dap'}, dimensions={0} | all-to-all | bytes 589824 | tf_op jit(solution)/shard_map/all_to_all | solution.py:200
  27.3 0.4 shard_map.65
  27.8 0.1 reshape.19
  27.9 16.5 %all_to_all.21 = f16[64,2,576]{2,1,0:T(2,128)(2,1)S(1)} all-to-all(f16[64,2,576]{2,1,0:T(2,128)(2,1)S(1)} %reshape.19), channel_id=1, replica_groups=mesh['crop'=4,'dap'=64] {'dap'}, dimensions={0} | all-to-all | bytes 294912 | tf_op jit(solution)/shard_map/all_to_all | solution.py:204
  44.4 0.7 shard_map.66
  45.2 0.1 reshape.20
  45.3 17.8 %all_to_all.22 = bf16[64,2,1152]{2,1,0:T(2,128)(2,1)S(1)} all-to-all(bf16[64,2,1152]{2,1,0:T(2,128)(2,1)S(1)} %reshape.20), channel_id=1, replica_groups=mesh['crop'=4,'dap'=64] {'dap'}, dimensions={0} | all-to-all | bytes 589824 | tf_op jit(solution)/shard_map/all_to_all | solution.py:200
  63.1 0.4 shard_map.67
  63.6 0.1 reshape.21
  63.7 16.5 %all_to_all.23 = f16[64,2,576]{2,1,0:T(2,128)(2,1)S(1)} all-to-all(f16[64,2,576]{2,1,0:T(2,128)(2,1)S(1)} %reshape.21), channel_id=1, replica_groups=mesh['crop'=4,'dap'=64] {'dap'}, dimensions={0} | all-to-all | bytes 294912 | tf_op jit(solution)/shard_map/all_to_all | solution.py:204
  80.3 1.1 %shard_map.68 = f32[3,192,128]{2,1,0:T(8,128)} custom-call(f32[128,576]{1,0:T(8,128)S(1)} %bitcast.15, f32[128,576]{1,0:T(8,128)S(1)} %get-tuple-element.31.state, f32[128,576]{1,0:T(8,128)S(1)} %get-tuple-element.32.gate, f32[2,128,128]{2,1,0:T(8,128)S(1)} %get-tuple-element.28.gains, bf16[2,128,128]{2,1,0:T(8,128)(2,1)S(1)} %get-tuple-element.29.w_out), custom_call_target="tpu_custom_call" | custom-call | tf_op jit(solution)/shard_map/pallas_call | solution.py:189
  (8 shorter events, 0.3 us)

commit v7 on v6

v7 whole, which is shorter than its diff:
```python
import jax
import jax.numpy as jnp
from jax import lax
from jax.experimental import pallas as pl
from jax.experimental.pallas import tpu as pltpu
from jax.sharding import PartitionSpec as P

F32 = jnp.float32
BF16 = jnp.bfloat16
LANES = 128
TOP = 2.0**14


def column(row):
    return jnp.transpose(jnp.broadcast_to(row, (8, row.shape[1])))[:, 0:1]


def norm_rows(value, gain):
    mean = jnp.mean(value, axis=0, keepdims=True)
    cent = value - mean
    var = jnp.mean(cent * cent, axis=0, keepdims=True)
    return (cent * lax.rsqrt(var + 1e-05) * gain).astype(BF16)


def mix(weight, value):
    return lax.dot_general(weight, value, (((0,), (0,)), ((), ())), preferred_element_type=F32)


def sigmoid(value):
    return 0.5 * jnp.tanh(0.5 * value) + 0.5


def blocks(rows):
    return [(k, j) for k in range(rows) for j in range(rows - 1)] + [
        (k, rows - 1) for k in range(rows)
    ]


def store_edges(both, proj):
    hidden = proj[0].shape[0] // 2
    left, right = ((sigmoid(p[:hidden]) * p[hidden:]).astype(BF16) for p in proj)
    whole = left.shape[1] // LANES * LANES
    both[:, :whole] = left[:, :whole]
    both[:, whole : whole + LANES] = jnp.concatenate([left[:, whole:], right[:, whole:]], axis=1)
    both[:, whole + LANES :] = right[:, :whole]


def first_kernel(
    pair,
    norm_in,
    w_proj,
    w_gate,
    norm_mid,
    w_out,
    both,
    normed,
    state,
    norm_in_near,
    w_proj_near,
    w_gate_near,
    norm_mid_near,
    w_out_near,
    pair_near,
    sems,
):
    rows, cols, chans = pair.shape
    half = cols // 2
    pairs = [
        (norm_in, norm_in_near),
        *((pair.at[k, pl.ds(h, half)], pair_near.at[k, pl.ds(h, half)]) for k in range(rows) for h in (0, half)),
        (w_proj.at[0], w_proj_near.at[0]),
        (w_gate, w_gate_near),
        (w_proj.at[1], w_proj_near.at[1]),
        (norm_mid, norm_mid_near),
        (w_out, w_out_near),
    ]
    moves = [pltpu.make_async_copy(*ends, sems.at[k]) for k, ends in enumerate(pairs)]
    for move in moves:
        move.start()
    for move in moves[:7]:
        move.wait()
    parts = cols // rows
    value = jnp.transpose(
        jnp.concatenate(
            [
                pair_near[k, pl.ds(j, parts, stride=rows), :] for k, j in blocks(rows)
            ],
            axis=0,
        )
    )
    state[...] = value
    gain = column(norm_in_near[0:1, :])
    moves[7].wait()
    normed[...] = norm_rows(value, gain)
    proj = mix(w_proj_near[0], normed[...])
    store_edges(both, (proj[: 2 * chans], proj[2 * chans :]))
    for move in moves[8:]:
        move.wait()


def middle_kernel(
    got, state, gate, norm_in, w_proj, gains, units, w_out, both, normed, state_next
):
    mid = norm_rows(got[...] * units[0][:, 0:1], gains[0][:, 0:1])
    value = state[...] + gate[...] * mix(w_out[0], mid)
    state_next[...] = value
    normed[...] = norm_rows(value, column(norm_in[1:2, :]))
    wide = w_proj.shape[2] // 2
    store_edges(both, [mix(w_proj[1][:, k : k + wide], normed[...]) for k in (0, wide)])


def last_kernel(got, state, gate, gains, units, w_out, out, near, sems):
    rows, cols, chans = out.shape
    parts = cols // rows
    gain = gains[1][:, 0:1]
    unit = units[1][:, 0:1]
    order = blocks(rows)
    moves = []
    for k, stop in ((0, rows - 1), (rows - 1, rows)):
        mine = [n for n, (row, _) in enumerate(order) if k <= row < stop]

        def lanes(ref):
            return jnp.concatenate([ref[:, n * parts : (n + 1) * parts] for n in mine], axis=1)

        value = lanes(state) + lanes(gate) * mix(w_out[1], norm_rows(lanes(got) * unit, gain))
        turned = jnp.transpose(value)
        for place, n in enumerate(mine):
            row, slot = order[n]
            near[row, pl.ds(slot, parts, stride=rows), :] = turned[
                place * parts : (place + 1) * parts
            ]
        block = pl.ds(k, stop - k)
        move = pltpu.make_async_copy(near.at[block], out.at[block], sems.at[len(moves)])
        move.start()
        moves.append(move)
    for move in moves:
        move.wait()


def square(value, whole, last):
    rows = [value[:, k : k + LANES] for k in range(whole, whole + 3 * LANES, LANES)]
    tail = value[:, whole + 3 * LANES : whole + 4 * LANES]
    half = LANES // 2
    tails = [tail[:, :half], tail[:, half:], last]
    return jnp.concatenate(
        [jnp.concatenate([row, end], axis=1) for row, end in zip(rows, tails)], axis=0
    )


def product(got, scales, out, tiles, dims):
    chans, parts, lanes = got.shape
    places = lanes // 2
    whole = places // LANES * LANES
    spare = jnp.zeros((parts, LANES - parts), F32)
    first = chans * lax.axis_index("dap")
    for chan in range(chans):
        value = got[chan]
        middle = value[:, whole : whole + LANES]
        left = square(value, 0, middle[:, :parts])
        right = square(value, whole + LANES, middle[:, parts:])
        tri = lax.dot_general(left, right, (dims, ((), ())), preferred_element_type=F32)
        tri = [tri[k : k + parts] for k in range(0, tri.shape[0], parts)]
        ends = [row[:, LANES:] for row in tri] + [spare]
        pieces = [row[:, :LANES] for row in tri]
        pieces += [jnp.concatenate(ends[k : k + 2], axis=1) for k in (0, 2)]
        scale = scales[pl.ds(first + chan, 1), :]
        for k, piece in enumerate(pieces):
            tiles[k, pl.ds(chan, parts, stride=chans), :] = piece * scale
    tri = jnp.concatenate([tiles[k] for k in range(tiles.shape[0])], axis=1)
    out[...] = tri[:, :places]


def largest(gain, w_proj, cols):
    hidden = w_proj.shape[1] // 4
    weighted = [
        gain * w_proj[:, k : k + hidden].astype(F32) for k in (hidden, 3 * hidden)
    ]
    left, right = (jnp.sum(w * w, axis=0, keepdims=True) for w in weighted)
    return 1.02 * cols * hidden * jnp.sqrt(left * right) + 1e-20


def outgoing_kernel(
    got,
    normed,
    norm_in,
    w_proj,
    w_gate,
    norm_mid,
    w_out,
    out,
    gate,
    gains,
    units,
    w_out_turned,
    scales,
    tiles,
    scratch,
):
    parts = got.shape[1]
    cols = 3 * parts
    half = scratch.shape[0] // 2

    def wide(row):
        return jnp.transpose(jnp.broadcast_to(row, scratch.shape))

    def turn(value, turned, which):
        scratch[...] = value
        for slot in range(2):
            turned[which, slot * half : (slot + 1) * half] = scratch[
                pl.ds(slot, half, stride=2), :
            ].astype(turned.dtype)

    for which in range(2):
        bound = largest(wide(norm_in[which : which + 1, :]), w_proj[which], cols)
        scales[which] = wide(TOP / bound)
        turn(wide(bound * (1 / TOP)), units, which)
        turn(wide(norm_mid[which : which + 1, :]), gains, which)
        turn(w_out[which].astype(F32), w_out_turned, which)
    product(got, scales.at[0], out, tiles, ((1,), (1,)))
    gate[...] = sigmoid(mix(w_gate[0], normed[...]))


def incoming_kernel(got, normed, w_gate, scales, out, gate, tiles):
    product(got, scales.at[1], out, tiles, ((0,), (0,)))
    gate[...] = sigmoid(mix(w_gate[1], normed[...]))


def per_device(pair, norm_in, w_proj, w_gate, norm_mid, w_out):
    rows, cols, chans = pair.shape
    parts = cols // rows
    places = rows * cols
    both_t = jax.ShapeDtypeStruct((chans, 2 * places), BF16)
    tri_t = jax.ShapeDtypeStruct((chans, places), F32)
    tiles = pltpu.VMEM((pl.cdiv(places, LANES), chans, LANES), F32)
    flat_t = jax.ShapeDtypeStruct((chans, places), F32)
    normed_t = jax.ShapeDtypeStruct((chans, places), BF16)
    near = pl.BlockSpec(memory_space=pltpu.VMEM)
    far = pl.BlockSpec(memory_space=pl.ANY)
    dma = pltpu.SemaphoreType.DMA

    def call(kernel, ins, outs, scratch=(), in_spec=near, out_spec=near):
        return pl.pallas_call(
            kernel,
            in_specs=[in_spec] * len(ins),
            out_specs=[out_spec] * len(outs),
            out_shape=outs,
            scratch_shapes=scratch,
            compiler_params=pltpu.CompilerParams(vmem_limit_bytes=32 * 2**20),
        )(*ins)

    def to_channels(both):
        both = both.reshape(parts, 2, 2 * places)
        return jnp.swapaxes(lax.all_to_all(both, "dap", 0, 0, tiled=True), 0, 1)

    def to_rows(tri):
        tri = tri.astype(jnp.float16).reshape(parts, 2, places)
        tri = jnp.swapaxes(lax.all_to_all(tri, "dap", 0, 0, tiled=True), 0, 1)
        tri = lax.optimization_barrier(tri)
        return tri.astype(F32).reshape(chans, places)

    def like(array):
        return jax.ShapeDtypeStruct(array.shape, array.dtype)

    params = (norm_in, w_proj, w_gate, norm_mid, w_out)
    both, normed, state, norm_in, w_proj, w_gate, norm_mid, w_out = call(
        first_kernel,
        tuple(pltpu.with_memory_space_constraint(a, pltpu.HBM) for a in (pair, *params)),
        [both_t, normed_t, flat_t, *map(like, params)],
        [pltpu.VMEM(pair.shape, F32), dma((12,))],
        in_spec=far,
    )
    wide_t = jax.ShapeDtypeStruct(w_out.shape, F32)
    tri, gate, gains, units, w_out, scales = call(
        outgoing_kernel,
        (to_channels(both), normed, norm_in, w_proj, w_gate, norm_mid, w_out),
        [tri_t, flat_t, wide_t, wide_t, like(w_out), wide_t],
        [tiles, pltpu.VMEM(w_out.shape[1:], F32)],
    )
    both, normed, state = call(
        middle_kernel,
        (to_rows(tri), state, gate, norm_in, w_proj, gains, units, w_out),
        [both_t, normed_t, flat_t],
    )
    tri, gate = call(
        incoming_kernel, (to_channels(both), normed, w_gate, scales), [tri_t, flat_t], [tiles]
    )
    (out,) = call(
        last_kernel,
        (to_rows(tri), state, gate, gains, units, w_out),
        [like(pair)],
        [pltpu.VMEM(pair.shape, F32), dma((2,))],
        out_spec=far,
    )
    return out


def solution(mesh):
    return jax.shard_map(
        per_device,
        mesh=mesh,
        in_specs=(P(("crop", "dap"), None, None), P(), P(), P(), P(), P()),
        out_specs=P(("crop", "dap"), None, None),
        check_vma=False,
    )
```

time: 81.6 us -> 81.7 us (level)
  no operation moved by 1% of the time
where the time goes in v7:
time: 81.7 us; the launch traced here: 81.5 us
  blocking collectives  76.2 us (93%)
  Pallas kernels  4.52 us (6%)
    all_to_all x2, blocking collectives, to_channels(): return jnp.swapaxes(lax.all_to_all(both, 'dap', 0, 0, tiled=True), 0, 1)  43.2 us
    all_to_all x2, blocking collectives, to_rows(): tri = jnp.swapaxes(lax.all_to_all(tri, 'dap', 0, 0, tiled=True), 0, 1)  32.9 us
    pallas_call x5, Pallas kernels, call(): pl.pallas_call(kernel, in_specs=[in_spec] * len(ins), out_specs=[out_spec...  4.52 us

profile of v7, /device:TPU:1, one launch (start us, length us, event | category | flops | bytes accessed | tf_op | source)
XLA Modules:
  0.0 81.5 jit_solution(10221894812930947746)
XLA Ops:
  0.0 1.7 %shard_map.64 = (bf16[128,1152]{1,0:T(8,128)(2,1)S(1)}, bf16[128,576]{1,0:T(8,128)(2,1)S(1)}, f32[128,576]{1,0:T(8,128)S(1)}, f32[2,128]{1,0:T(2,128)S(1)}, bf16...) custom-call(f32[3,192,128]{2,1,0:T(8,128)} %pair.1, ...), custom_call_target="tpu_custom_call" | custom-call | tf_op jit(solution)/shard_map/pallas_call | solution.py:242
  1.7 0.1 reshape.22
  1.8 25.4 %all_to_all.20 = bf16[64,2,1152]{2,1,0:T(2,128)(2,1)S(1)} all-to-all(bf16[64,2,1152]{2,1,0:T(2,128)(2,1)S(1)} %reshape.22), channel_id=1, replica_groups=mesh['crop'=4,'dap'=64] {'dap'}, dimensions={0} | all-to-all | bytes 589824 | tf_op jit(solution)/shard_map/all_to_all | solution.py:253
  27.3 0.5 shard_map.65
  27.8 0.1 reshape.23
  27.9 16.5 %all_to_all.21 = f16[64,2,576]{2,1,0:T(2,128)(2,1)S(1)} all-to-all(f16[64,2,576]{2,1,0:T(2,128)(2,1)S(1)} %reshape.23), channel_id=1, replica_groups=mesh['crop'=4,'dap'=64] {'dap'}, dimensions={0} | all-to-all | bytes 294912 | tf_op jit(solution)/shard_map/all_to_all | solution.py:257
  44.5 0.8 shard_map.66
  45.3 0.1 reshape.26
  45.4 17.8 %all_to_all.22 = bf16[64,2,1152]{2,1,0:T(2,128)(2,1)S(1)} all-to-all(bf16[64,2,1152]{2,1,0:T(2,128)(2,1)S(1)} %reshape.26), channel_id=1, replica_groups=mesh['crop'=4,'dap'=64] {'dap'}, dimensions={0} | all-to-all | bytes 589824 | tf_op jit(solution)/shard_map/all_to_all | solution.py:253
  63.2 0.4 shard_map.67
  63.6 0.1 reshape.27
  63.7 16.5 %all_to_all.23 = f16[64,2,576]{2,1,0:T(2,128)(2,1)S(1)} all-to-all(f16[64,2,576]{2,1,0:T(2,128)(2,1)S(1)} %reshape.27), channel_id=1, replica_groups=mesh['crop'=4,'dap'=64] {'dap'}, dimensions={0} | all-to-all | bytes 294912 | tf_op jit(solution)/shard_map/all_to_all | solution.py:257
  80.3 1.2 %shard_map.68 = f32[3,192,128]{2,1,0:T(8,128)} custom-call(f32[128,576]{1,0:T(8,128)S(1)} %bitcast_convert_fusion.got, f32[128,576]{1,0:T(8,128)S(1)} %get-tuple-element.41.state, f32[128,576]{1,0:T(8,128)S(1)} %get-tuple-element.42.gate, f32[2,128,128]{2,1,0:T(8,128)S(1)} %get-tuple-element.34.gains, f32[2,128,128]{2,1,0:T(8,128)S(1)} %get-tuple-element.35.units, ...), custom_call_target="tpu_custom_call" | custom-call | tf_op jit(solution)/shard_map/pallas_call | solution.py:242
  (8 shorter events, 0.3 us)

commit v8 on v4

v8 whole, which is shorter than its diff:
```python
import jax
import jax.numpy as jnp
from jax import lax
from jax.experimental import pallas as pl
from jax.experimental.pallas import tpu as pltpu
from jax.sharding import PartitionSpec as P

F32 = jnp.float32
BF16 = jnp.bfloat16
LANES = 128
ROWS = 3
OWN = 2
TOP = 2.0**14


def blocks():
    return [(k, j) for k in range(ROWS) for j in range(ROWS - 1)] + [
        (k, ROWS - 1) for k in range(ROWS)
    ]


def wide(row):
    return jnp.transpose(jnp.broadcast_to(row, (row.shape[1], row.shape[1])))


def spread(tile, width):
    whole = [tile] * (width // LANES)
    rest = [tile[:, : width % LANES]] if width % LANES else []
    return jnp.concatenate(whole + rest, axis=1)


def norm_rows(value, gain):
    mean = jnp.mean(value, axis=0, keepdims=True)
    cent = value - mean
    var = jnp.mean(cent * cent, axis=0, keepdims=True)
    return (cent * lax.rsqrt(var + 1e-05) * spread(gain, value.shape[1])).astype(BF16)


def mix(weight, value):
    return lax.dot_general(weight, value, (((0,), (0,)), ((), ())), preferred_element_type=F32)


def sigmoid(value):
    return 0.5 * jnp.tanh(0.5 * value) + 0.5


def lane_tiles(value):
    return [value[:, k : k + LANES] for k in range(0, value.shape[1], LANES)]


def put(ref, tile, chan, value):
    parts = value.shape[0]
    ref[pl.ds(tile * OWN + chan, parts, stride=ref.shape[0] // parts), :] = value


def take(ref, tile, chan, parts):
    return ref[pl.ds(tile * OWN + chan, parts, stride=ref.shape[0] // parts), :]


def put_edges(both, proj):
    hidden = proj[0].shape[0] // 2
    parts = hidden // OWN
    left, right = (lane_tiles(sigmoid(p[:hidden]) * p[hidden:]) for p in proj)
    middle = jnp.concatenate([left[-1], right[-1]], axis=1)
    for k, tile in enumerate([*left[:-1], middle, *right[:-1]]):
        for chan in range(OWN):
            put(both, k, chan, tile[chan * parts : (chan + 1) * parts])


def first_kernel(
    pair,
    norm_in,
    w_proj,
    w_gate,
    norm_mid,
    w_out,
    both,
    normed,
    state,
    norm_in_near,
    w_proj_near,
    w_gate_near,
    norm_mid_near,
    w_out_near,
    pair_near,
    sems,
):
    cols, chans = pair.shape[1:]
    half = cols // 2
    parts = cols // ROWS
    ends = [(norm_in, norm_in_near)]
    for k in range(ROWS):
        for h in (0, half):
            ends.append((pair.at[k, pl.ds(h, half)], pair_near.at[k, pl.ds(h, half)]))
    ends += [
        (w_proj.at[0], w_proj_near.at[0]),
        (w_gate, w_gate_near),
        (w_proj.at[1], w_proj_near.at[1]),
        (norm_mid, norm_mid_near),
        (w_out, w_out_near),
    ]
    moves = [pltpu.make_async_copy(*pair_of, sems.at[k]) for k, pair_of in enumerate(ends)]
    for move in moves:
        move.start()
    for move in moves[:7]:
        move.wait()
    value = jnp.transpose(
        jnp.concatenate(
            [pair_near[k, pl.ds(j, parts, stride=ROWS), :] for k, j in blocks()], axis=0
        )
    )
    state[...] = value
    gain = wide(norm_in_near[0:1, :])
    moves[7].wait()
    normed[...] = norm_rows(value, gain)
    proj = mix(w_proj_near[0], normed[...])
    put_edges(both, (proj[: 2 * chans], proj[2 * chans :]))
    for move in moves[8:]:
        move.wait()


def middle_kernel(got, state, gate, w_proj, gains, units, w_out, both, normed, state_next):
    chans, places = state.shape
    parts = chans // OWN
    tri = [
        jnp.concatenate([take(got, k, chan, parts) for chan in range(OWN)], axis=0)
        for k in range(pl.cdiv(places, LANES))
    ]
    tri = jnp.concatenate([tile * units[0] for tile in tri], axis=1)[:, :places]
    value = state[...] + gate[...] * mix(w_out[0], norm_rows(tri, gains[0]))
    state_next[...] = value
    normed[...] = norm_rows(value, gains[2])
    each = w_proj.shape[2] // 2
    put_edges(both, [mix(w_proj[1][:, k : k + each], normed[...]) for k in (0, each)])


def last_kernel(got, state, gate, gains, units, w_out, out, near, sems):
    cols, chans = out.shape[1:]
    parts = cols // ROWS
    order = blocks()
    moves = []
    for tiles, rows in (((0, 1, 3), (0, 1)), ((2, 4), (2,))):
        mine = [n for n in range(len(order)) if n // 2 in tiles]
        width = len(mine) * parts

        def lanes(ref):
            pieces = [ref[:, k * LANES : min((k + 1) * LANES, ref.shape[1])] for k in tiles]
            return jnp.concatenate(pieces, axis=1)

        tri = [
            jnp.concatenate([take(got, k, chan, parts) for chan in range(OWN)], axis=0)
            for k in tiles
        ]
        tri = jnp.concatenate([tile * units[1] for tile in tri], axis=1)[:, :width]
        value = lanes(state) + lanes(gate) * mix(w_out[1], norm_rows(tri, gains[1]))
        turned = jnp.transpose(value)
        for place, n in enumerate(mine):
            row, slot = order[n]
            near[row, pl.ds(slot, parts, stride=ROWS), :] = turned[
                place * parts : (place + 1) * parts
            ]
        block = pl.ds(rows[0], len(rows))
        move = pltpu.make_async_copy(near.at[block], out.at[block], sems.at[len(moves)])
        move.start()
        moves.append(move)
    for move in moves:
        move.wait()


def square(mains, tail, last):
    half = LANES // 2
    tails = [tail[:, :half], tail[:, half:], last]
    rows = [jnp.concatenate([main, end], axis=1) for main, end in zip(mains, tails)]
    return jnp.concatenate(rows, axis=0).astype(BF16)


def product(got, scales, out, dims):
    parts = scales.shape[0] // OWN
    half = LANES // 2
    me = lax.axis_index("dap")
    for chan in range(OWN):
        tiles = [take(got, k, chan, parts) for k in range(9)]
        left = square(tiles[:3], tiles[3], tiles[4][:, :half])
        right = square(tiles[5:8], tiles[8], tiles[4][:, half:])
        tri = lax.dot_general(left, right, (dims, ((), ())), preferred_element_type=F32)
        tri = [tri[k : k + parts] for k in range(0, tri.shape[0], parts)]
        ends = [row[:, LANES:] for row in tri] + [jnp.zeros((parts, half), F32)]
        tiles = [row[:, :LANES] for row in tri]
        tiles += [jnp.concatenate(ends[k : k + 2], axis=1) for k in (0, 2)]
        scale = scales[pl.ds(chan * parts + me, 1), :]
        for k, tile in enumerate(tiles):
            put(out, k, chan, tile * scale)


def largest(gain, w_proj, cols):
    hidden = w_proj.shape[1] // 4
    weighted = [gain * w_proj[:, k : k + hidden].astype(F32) for k in (hidden, 3 * hidden)]
    left, right = (jnp.sum(w * w, axis=0, keepdims=True) for w in weighted)
    return 1.02 * cols * hidden * jnp.sqrt(left * right) + 1e-20


def outgoing_kernel(
    got, normed, norm_in, w_proj, w_gate, norm_mid, out, gate, gains, units, scales
):
    cols = scales.shape[1] // OWN * ROWS
    for which in range(2):
        gain = wide(norm_in[which : which + 1, :])
        bound = largest(gain, w_proj[which], cols)
        scales[which] = wide(TOP / bound)
        units[which] = wide(bound * (1 / TOP))
        gains[which] = wide(norm_mid[which : which + 1, :])
    gains[2] = gain
    product(got, scales.at[0], out, ((1,), (1,)))
    gate[...] = sigmoid(mix(w_gate[0], normed[...]))


def incoming_kernel(got, normed, w_gate, scales, out, gate):
    product(got, scales.at[1], out, ((0,), (0,)))
    gate[...] = sigmoid(mix(w_gate[1], normed[...]))


def per_device(pair, norm_in, w_proj, w_gate, norm_mid, w_out):
    cols, chans = pair.shape[1:]
    parts = cols // ROWS
    places = ROWS * cols
    tiles = pl.cdiv(places, LANES)
    both_t = jax.ShapeDtypeStruct((parts * OWN * 2 * places // LANES, LANES), F32)
    tri_t = jax.ShapeDtypeStruct((parts * OWN * tiles, LANES), F32)
    flat_t = jax.ShapeDtypeStruct((chans, places), F32)
    normed_t = jax.ShapeDtypeStruct((chans, places), BF16)
    near = pl.BlockSpec(memory_space=pltpu.VMEM)
    far = pl.BlockSpec(memory_space=pl.ANY)
    dma = pltpu.SemaphoreType.DMA

    def call(kernel, ins, outs, scratch=(), in_spec=near, out_spec=near):
        return pl.pallas_call(
            kernel,
            in_specs=[in_spec] * len(ins),
            out_specs=[out_spec] * len(outs),
            out_shape=outs,
            scratch_shapes=scratch,
            compiler_params=pltpu.CompilerParams(vmem_limit_bytes=32 * 2**20),
        )(*ins)

    def exchange(value, kind):
        sent = value.astype(kind).reshape(parts, -1, OWN, LANES)
        got = lax.all_to_all(sent, "dap", 0, 0, tiled=True)
        return got.reshape(value.shape).astype(F32)

    def like(array):
        return jax.ShapeDtypeStruct(array.shape, array.dtype)

    def squares(count):
        return jax.ShapeDtypeStruct((count, chans, chans), F32)

    params = (norm_in, w_proj, w_gate, norm_mid, w_out)
    both, normed, state, norm_in, w_proj, w_gate, norm_mid, w_out = call(
        first_kernel,
        tuple(pltpu.with_memory_space_constraint(a, pltpu.HBM) for a in (pair, *params)),
        [both_t, normed_t, flat_t, *map(like, params)],
        [pltpu.VMEM(pair.shape, F32), dma((12,))],
        in_spec=far,
    )
    tri, gate, gains, units, scales = call(
        outgoing_kernel,
        (exchange(both, BF16), normed, norm_in, w_proj, w_gate, norm_mid),
        [tri_t, flat_t, squares(3), squares(2), squares(2)],
    )
    both, normed, state = call(
        middle_kernel,
        (exchange(tri, jnp.float16), state, gate, w_proj, gains, units, w_out),
        [both_t, normed_t, flat_t],
    )
    tri, gate = call(
        incoming_kernel, (exchange(both, BF16), normed, w_gate, scales), [tri_t, flat_t]
    )
    (out,) = call(
        last_kernel,
        (exchange(tri, jnp.float16), state, gate, gains, units, w_out),
        [like(pair)],
        [pltpu.VMEM(pair.shape, F32), dma((2,))],
        out_spec=far,
    )
    return out


def solution(mesh):
    return jax.shard_map(
        per_device,
        mesh=mesh,
        in_specs=(P(("crop", "dap"), None, None), P(), P(), P(), P(), P()),
        out_specs=P(("crop", "dap"), None, None),
        check_vma=False,
    )
```

time: 82.3 us -> 81 us (0.984)
  local copies, waits for them, and re-layouts: 1.06 us -> 0 us
    pallas_call x4 -> x0, local copies, waits for them, and re-layouts: 0.95 us -> none  [call(): pl.pallas_call(kernel, in_specs=[in_spec] * len(ins), out_specs=[out_spec...]
where the time goes in v8:
time: 81 us; the launch traced here: 80.7 us
  blocking collectives  76.2 us (94%)
  Pallas kernels  4.24 us (5%)
    all_to_all x4, blocking collectives, exchange(): got = lax.all_to_all(sent, 'dap', 0, 0, tiled=True)  76.2 us
    pallas_call x5, Pallas kernels, call(): pl.pallas_call(kernel, in_specs=[in_spec] * len(ins), out_specs=[out_spec...  4.24 us

profile of v8, /device:TPU:1, one launch (start us, length us, event | category | flops | bytes accessed | tf_op | source)
XLA Modules:
  0.0 80.7 jit_solution(6240483581871825188)
XLA Ops:
  0.0 1.7 %shard_map.64 = (f32[1152,128]{1,0:T(8,128)S(1)}, bf16[128,576]{1,0:T(8,128)(2,1)S(1)}, f32[128,576]{1,0:T(8,128)S(1)}, f32[2,128]{1,0:T(2,128)S(1)}, bf16[2,128...) custom-call(f32[3,192,128]{2,1,0:T(8,128)} %pair.1, ...), custom_call_target="tpu_custom_call" | custom-call | tf_op jit(solution)/shard_map/pallas_call | solution.py:236
  1.7 25.4 %all_to_all.20 = bf16[64,9,2,128]{3,2,1,0:T(2,128)(2,1)S(1)} all-to-all(bf16[64,9,2,128]{3,2,1,0:T(2,128)(2,1)S(1)} %bitcast.12), channel_id=1, replica_groups=mesh['crop'=4,'dap'=64] {'dap'}, dimensions={0} | all-to-all | bytes 589824 | tf_op jit(solution)/shard_map/all_to_all | solution.py:247
  27.2 0.4 shard_map.65
  27.6 16.5 %all_to_all.21 = f16[64,5,2,128]{3,2,1,0:T(2,128)(2,1)S(1)} all-to-all(f16[64,5,2,128]{3,2,1,0:T(2,128)(2,1)S(1)} %bitcast.16), channel_id=1, replica_groups=mesh['crop'=4,'dap'=64] {'dap'}, dimensions={0} | all-to-all | bytes 327680 | tf_op jit(solution)/shard_map/all_to_all | solution.py:247
  44.1 0.7 shard_map.66
  44.9 17.8 %all_to_all.22 = bf16[64,9,2,128]{3,2,1,0:T(2,128)(2,1)S(1)} all-to-all(bf16[64,9,2,128]{3,2,1,0:T(2,128)(2,1)S(1)} %bitcast.14), channel_id=1, replica_groups=mesh['crop'=4,'dap'=64] {'dap'}, dimensions={0} | all-to-all | bytes 589824 | tf_op jit(solution)/shard_map/all_to_all | solution.py:247
  62.8 0.4 shard_map.67
  63.2 16.5 %all_to_all.23 = f16[64,5,2,128]{3,2,1,0:T(2,128)(2,1)S(1)} all-to-all(f16[64,5,2,128]{3,2,1,0:T(2,128)(2,1)S(1)} %bitcast.18), channel_id=1, replica_groups=mesh['crop'=4,'dap'=64] {'dap'}, dimensions={0} | all-to-all | bytes 327680 | tf_op jit(solution)/shard_map/all_to_all | solution.py:247
  79.6 1.1 %shard_map.68 = f32[3,192,128]{2,1,0:T(8,128)} custom-call(f32[640,128]{1,0:T(8,128)S(1)} %convert.7.got, f32[128,576]{1,0:T(8,128)S(1)} %get-tuple-element.39.state, f32[128,576]{1,0:T(8,128)S(1)} %get-tuple-element.40.gate, f32[3,128,128]{2,1,0:T(8,128)S(1)} %get-tuple-element.32.gains, f32[2,128,128]{2,1,0:T(8,128)S(1)} %get-tuple-element.33.units, ...), custom_call_target="tpu_custom_call" | custom-call | tf_op jit(solution)/shard_map/pallas_call | solution.py:236
  (8 shorter events, 0.2 us)

commit v9 on v8

v9 whole, which is shorter than its diff:
```python
import jax
import jax.numpy as jnp
from jax import lax
from jax.experimental import pallas as pl
from jax.experimental.pallas import tpu as pltpu
from jax.sharding import Mesh
from jax.sharding import PartitionSpec as P

F32 = jnp.float32
BF16 = jnp.bfloat16
LANES = 128
ROWS = 3
OWN = 4
CORES = 2
TOP = 2.0**14


def blocks():
    return [(k, j) for k in range(ROWS) for j in range(ROWS - 1)] + [
        (k, ROWS - 1) for k in range(ROWS)
    ]


def wide(row):
    return jnp.transpose(jnp.broadcast_to(row, (row.shape[1], row.shape[1])))


def spread(tile, width):
    whole = [tile] * (width // LANES)
    rest = [tile[:, : width % LANES]] if width % LANES else []
    return jnp.concatenate(whole + rest, axis=1)


def norm_rows(value, gain):
    mean = jnp.mean(value, axis=0, keepdims=True)
    cent = value - mean
    var = jnp.mean(cent * cent, axis=0, keepdims=True)
    return (cent * lax.rsqrt(var + 1e-05) * spread(gain, value.shape[1])).astype(BF16)


def mix(weight, value):
    return lax.dot_general(weight, value, (((0,), (0,)), ((), ())), preferred_element_type=F32)


def sigmoid(value):
    return 0.5 * jnp.tanh(0.5 * value) + 0.5


def lane_tiles(value):
    return [value[:, k : k + LANES] for k in range(0, value.shape[1], LANES)]


def put(ref, row, value):
    ref[pl.ds(row, value.shape[0], stride=ref.shape[0] // value.shape[0]), :] = value


def take(ref, row, parts):
    return ref[pl.ds(row, parts, stride=ref.shape[0] // parts), :]


def put_tiles(ref, tiles, first):
    for k in range(len(tiles[0]) - 1):
        for chan in range(OWN):
            put(ref, first + k * OWN + chan, tiles[chan][k])
    for pair in range(OWN // 2):
        halves = [tiles[2 * pair + k][-1] for k in range(2)]
        row = first + (len(tiles[0]) - 1) * OWN + pair
        put(ref, row, jnp.concatenate(halves, axis=1))


def take_tiles(ref, first, chan, parts):
    tiles = [take(ref, first + k * OWN + chan, parts) for k in range(4)]
    last = take(ref, first + 4 * OWN + chan // 2, parts)
    start = chan % 2 * (LANES // 2)
    return tiles + [last[:, start : start + LANES // 2]]


def take_rows(ref, tiles, parts):
    mine = [take_tiles(ref, 0, chan, parts) for chan in range(OWN)]
    return [jnp.concatenate([m[k] for m in mine], axis=0) for k in tiles]


def put_edges(both, proj):
    hidden = proj[0].shape[0] // 2
    parts = hidden // OWN
    for side, p in enumerate(proj):
        edge = sigmoid(p[:hidden]) * p[hidden:]
        tiles = [lane_tiles(edge[k : k + parts]) for k in range(0, hidden, parts)]
        put_tiles(both, tiles, side * 18)


def first_kernel(
    pair,
    norm_in,
    w_proj,
    w_gate,
    norm_mid,
    w_out,
    both,
    normed,
    state,
    norm_in_near,
    w_proj_near,
    w_gate_near,
    norm_mid_near,
    w_out_near,
    pair_near,
    sems,
):
    cols, chans = pair.shape[1:]
    half = cols // 2
    parts = cols // (ROWS * CORES)
    ends = [(norm_in, norm_in_near)]
    for k in range(ROWS):
        for h in (0, half):
            ends.append((pair.at[k, pl.ds(h, half)], pair_near.at[k, pl.ds(h, half)]))
    ends += [
        (w_proj.at[0], w_proj_near.at[0]),
        (w_gate, w_gate_near),
        (w_proj.at[1], w_proj_near.at[1]),
        (norm_mid, norm_mid_near),
        (w_out, w_out_near),
    ]
    moves = [pltpu.make_async_copy(*pair_of, sems.at[k]) for k, pair_of in enumerate(ends)]
    for move in moves:
        move.start()
    for move in moves[:7]:
        move.wait()
    value = jnp.transpose(
        jnp.concatenate(
            [
                pair_near[k, pl.ds(core * ROWS + j, parts, stride=CORES * ROWS), :]
                for k, j in blocks()
                for core in range(CORES)
            ],
            axis=0,
        )
    )
    state[...] = value
    gain = wide(norm_in_near[0:1, :])
    moves[7].wait()
    normed[...] = norm_rows(value, gain)
    proj = mix(w_proj_near[0], normed[...])
    put_edges(both, (proj[: 2 * chans], proj[2 * chans :]))
    for move in moves[8:]:
        move.wait()


def middle_kernel(got, state, gate, w_proj, gains, units, w_out, both, normed, state_next):
    chans, places = state.shape
    parts = chans // OWN
    tri = take_rows(got, range(5), parts)
    tri = jnp.concatenate(tri, axis=1) * spread(units[0], places)
    value = state[...] + gate[...] * mix(w_out[0], norm_rows(tri, gains[0]))
    state_next[...] = value
    normed[...] = norm_rows(value, gains[2])
    each = w_proj.shape[2] // 2
    put_edges(both, [mix(w_proj[1][:, k : k + each], normed[...]) for k in (0, each)])


def last_kernel(got, state, gate, gains, units, w_out, out, near, sems):
    cols, chans = out.shape[1:]
    parts = cols // (ROWS * CORES)
    order = [(k, core * ROWS + j) for k, j in blocks() for core in range(CORES)]
    moves = []
    for tiles, rows in (((0, 1, 3), (0, 1)), ((2, 4), (2,))):
        mine = [n for n in range(len(order)) if n // (2 * CORES) in tiles]
        width = len(mine) * parts

        def lanes(ref):
            pieces = [ref[:, k * LANES : min((k + 1) * LANES, ref.shape[1])] for k in tiles]
            return jnp.concatenate(pieces, axis=1)

        tri = jnp.concatenate(take_rows(got, tiles, parts), axis=1) * spread(units[1], width)
        value = lanes(state) + lanes(gate) * mix(w_out[1], norm_rows(tri, gains[1]))
        turned = jnp.transpose(value)
        for place, n in enumerate(mine):
            row, slot = order[n]
            near[row, pl.ds(slot, parts, stride=CORES * ROWS), :] = turned[
                place * parts : (place + 1) * parts
            ]
        block = pl.ds(rows[0], len(rows))
        move = pltpu.make_async_copy(near.at[block], out.at[block], sems.at[len(moves)])
        move.start()
        moves.append(move)
    for move in moves:
        move.wait()


def square(tiles):
    half = LANES // 2
    tails = [tiles[3][:, :half], tiles[3][:, half:], tiles[4]]
    return [jnp.concatenate([main, end], axis=1) for main, end in zip(tiles[:3], tails)]


def stack(rows):
    return jnp.concatenate(rows, axis=0).astype(BF16)


def product_tiles(rows, scale):
    tails = [row[:, LANES:] for row in rows]
    tiles = [row[:, :LANES] * scale for row in rows]
    tiles.append(jnp.concatenate(tails[:2], axis=1) * scale)
    return tiles + [tails[2] * scale[:, : LANES // 2]]


def scale_of(scales, chan):
    parts = scales.shape[0] // OWN
    return scales[pl.ds(chan * parts + lax.axis_index("chip"), 1), :]


def largest(gain, w_proj, cols):
    hidden = w_proj.shape[1] // 4
    weighted = [gain * w_proj[:, k : k + hidden].astype(F32) for k in (hidden, 3 * hidden)]
    left, right = (jnp.sum(w * w, axis=0, keepdims=True) for w in weighted)
    return 1.02 * cols * hidden * jnp.sqrt(left * right) + 1e-20


def outgoing_kernel(
    got, other, normed, norm_in, w_proj, w_gate, norm_mid, out, gate, gains, units, scales
):
    parts = scales.shape[1] // OWN
    for which in range(2):
        gain = wide(norm_in[which : which + 1, :])
        bound = largest(gain, w_proj[which], parts * CORES * ROWS)
        scales[which] = wide(TOP / bound)
        units[which] = wide(bound * (1 / TOP))
        gains[which] = wide(norm_mid[which : which + 1, :])
    gains[2] = gain
    first = lax.axis_index("core") == 0
    tiles = []
    for chan in range(OWN):
        left = stack(square(take_tiles(got, 0, chan, parts)))
        own = square(take_tiles(got, 18, chan, parts))
        far = square(take_tiles(other, 0, chan, parts))
        right = []
        for mine, theirs in zip(own, far):
            right += [jnp.where(first, mine, theirs), jnp.where(first, theirs, mine)]
        tri = lax.dot_general(
            left, stack(right), (((1,), (1,)), ((), ())), preferred_element_type=F32
        )
        rows = [tri[k : k + parts] for k in range(0, tri.shape[0], parts)]
        tiles.append(product_tiles(rows, scale_of(scales.at[0], chan)))
    put_tiles(out, tiles, 0)
    gate[...] = sigmoid(mix(w_gate[0], normed[...]))


def incoming_kernel(got, normed, w_gate, scales, out, out_other, gate):
    parts = scales.shape[1] // OWN
    first = lax.axis_index("core") == 0
    kept, given = [], []
    for chan in range(OWN):
        left = stack(square(take_tiles(got, 0, chan, parts)))
        right = stack(square(take_tiles(got, 18, chan, parts)))
        tri = mix(left, right)
        rows = [tri[k : k + parts] for k in range(0, tri.shape[0], parts)]
        pairs = list(zip(rows[0::2], rows[1::2]))
        scale = scale_of(scales.at[1], chan)
        kept.append(product_tiles([jnp.where(first, a, b) for a, b in pairs], scale))
        given.append(product_tiles([jnp.where(first, b, a) for a, b in pairs], scale))
    put_tiles(out, kept, 0)
    put_tiles(out_other, given, 0)
    gate[...] = sigmoid(mix(w_gate[1], normed[...]))


def per_device(pair, norm_in, w_proj, w_gate, norm_mid, w_out):
    cols, chans = pair.shape[1:]
    parts = cols // (ROWS * CORES)
    places = ROWS * cols
    tri_t = jax.ShapeDtypeStruct((parts * OWN * places // LANES, LANES), F32)
    both_t = jax.ShapeDtypeStruct((2 * tri_t.shape[0], LANES), F32)
    flat_t = jax.ShapeDtypeStruct((chans, places), F32)
    normed_t = jax.ShapeDtypeStruct((chans, places), BF16)
    near = pl.BlockSpec(memory_space=pltpu.VMEM)
    far = pl.BlockSpec(memory_space=pl.ANY)
    dma = pltpu.SemaphoreType.DMA

    def call(kernel, ins, outs, scratch=(), in_spec=near, out_spec=near):
        return pl.pallas_call(
            kernel,
            in_specs=[in_spec] * len(ins),
            out_specs=[out_spec] * len(outs),
            out_shape=outs,
            scratch_shapes=scratch,
            compiler_params=pltpu.CompilerParams(vmem_limit_bytes=32 * 2**20),
        )(*ins)

    def exchange(value):
        sent = value.reshape(parts, -1, 2, LANES)
        return lax.all_to_all(sent, "chip", 0, 0, tiled=True)

    def swap(value):
        return lax.ppermute(value, "core", [(0, 1), (1, 0)])

    def rows_of(value):
        return value.reshape(-1, LANES).astype(F32)

    def like(array):
        return jax.ShapeDtypeStruct(array.shape, array.dtype)

    def squares(count):
        return jax.ShapeDtypeStruct((count, chans, chans), F32)

    params = (norm_in, w_proj, w_gate, norm_mid, w_out)
    both, normed, state, norm_in, w_proj, w_gate, norm_mid, w_out = call(
        first_kernel,
        tuple(pltpu.with_memory_space_constraint(a, pltpu.HBM) for a in (pair, *params)),
        [both_t, normed_t, flat_t, *map(like, params)],
        [pltpu.VMEM(pair.shape, F32), dma((12,))],
        in_spec=far,
    )
    got = exchange(both.astype(BF16))
    other = swap(got[:, got.shape[1] // 2 :])
    tri, gate, gains, units, scales = call(
        outgoing_kernel,
        (rows_of(got), rows_of(other), normed, norm_in, w_proj, w_gate, norm_mid),
        [tri_t, flat_t, squares(3), squares(2), squares(2)],
    )
    got = exchange(tri.astype(jnp.float16))
    both, normed, state = call(
        middle_kernel,
        (rows_of(got), state, gate, w_proj, gains, units, w_out),
        [both_t, normed_t, flat_t],
    )
    got = exchange(both.astype(BF16))
    tri, given, gate = call(
        incoming_kernel, (rows_of(got), normed, w_gate, scales), [tri_t, tri_t, flat_t]
    )
    tri = tri + swap(given.astype(jnp.float16)).astype(F32)
    got = exchange(tri.astype(jnp.float16))
    (out,) = call(
        last_kernel,
        (rows_of(got), state, gate, gains, units, w_out),
        [like(pair)],
        [pltpu.VMEM(pair.shape, F32), dma((2,))],
        out_spec=far,
    )
    return out


def solution(mesh):
    crops, devices = mesh.devices.shape
    split = Mesh(mesh.devices.reshape(crops, devices // CORES, CORES), ("crop", "chip", "core"))
    whole = P(("crop", "chip", "core"), None, None)
    return jax.shard_map(
        per_device,
        mesh=split,
        in_specs=(whole, P(), P(), P(), P(), P()),
        out_specs=whole,
        check_vma=False,
    )
```

time: 81 us -> 78.6 us (0.970)
  blocking collectives: 76.2 us -> 62.6 us
  starting transfers between devices: 0 us -> 8.14 us
  waiting for transfers between devices: 0 us -> 1.97 us
    all_to_all x4, blocking collectives: 76.2 us -> 62.6 us  [exchange(): return lax.all_to_all(sent, 'chip', 0, 0, tiled=True)]
    ppermute x0 -> x2, starting transfers between devices: none -> 8.14 us  [swap(): return lax.ppermute(value, 'core', [(0, 1), (1, 0)])]
    ppermute x0 -> x2, waiting for transfers between devices: none -> 1.97 us  [swap(): return lax.ppermute(value, 'core', [(0, 1), (1, 0)])]
  transfers between devices with their start and end apart: 0 -> 2, of which waited for: 0 -> 2; matrix products, arithmetic and copies ran while one was open for 0% -> 0% of each run, Pallas kernels for 0% -> 0%
where the time goes in v9:
time: 78.6 us; the launch traced here: 77.6 us
  blocking collectives  62.6 us (80%)
  starting transfers between devices  8.14 us (10%)
  Pallas kernels  4.38 us (6%)
  waiting for transfers between devices  1.97 us (3%)
    all_to_all x4, blocking collectives, exchange(): return lax.all_to_all(sent, 'chip', 0, 0, tiled=True)  62.6 us
    ppermute x2, starting transfers between devices, swap(): return lax.ppermute(value, 'core', [(0, 1), (1, 0)])  8.14 us
    pallas_call x5, Pallas kernels, call(): pl.pallas_call(kernel, in_specs=[in_spec] * len(ins), out_specs=[out_spec...  4.38 us
    ppermute x2, waiting for transfers between devices, swap(): return lax.ppermute(value, 'core', [(0, 1), (1, 0)])  1.97 us
  transfers between devices with their start and end apart: 2, of which 2 were waited for; matrix products, arithmetic and copies ran while one was open for 0% of the time, Pallas kernels for 0%

profile of v9, /device:TPU:1, one launch (start us, length us, event | category | flops | bytes accessed | tf_op | source)
XLA Modules:
  0.0 77.6 jit_solution(11248503021163946187)
XLA Ops:
  0.0 1.7 %shard_map.64 = (f32[1152,128]{1,0:T(8,128)S(1)}, bf16[128,576]{1,0:T(8,128)(2,1)S(1)}, f32[128,576]{1,0:T(8,128)S(1)}, f32[2,128]{1,0:T(2,128)S(1)}, bf16[2,128...) custom-call(f32[3,192,128]{2,1,0:T(8,128)} %pair.1, ...), custom_call_target="tpu_custom_call" | custom-call | tf_op jit(solution)/shard_map/pallas_call | solution.py:279
  1.7 21.6 %all_to_all.20 = bf16[32,18,2,128]{3,2,1,0:T(2,128)(2,1)S(1)} all-to-all(bf16[32,18,2,128]{3,2,1,0:T(2,128)(2,1)S(1)} %bitcast.15), channel_id=1, replica_groups=mesh['crop'=4,'chip'=32,'core'=2] {'chip'}, dimensions={0} | all-to-all | bytes 589824 | tf_op jit(solution)/shard_map/all_to_all | solution.py:290
  23.3 0.1 slice.4
  23.4 4.0 %collective-permute-start = (bf16[32,9,2,128]{3,2,1,0:T(2,128)(2,1)S(1)}, bf16[32,9,2,128]{3,2,1,0:T(2,128)(2,1)S(1)}, u32[]{:S(2)}, u32[]{:S(2)}) collective-permute-start(bf16[32,9,2,128]{3,2,1,0:T(2,128)(2,1)S(1)} %slice.4), channel_id=1, source_target_pairs={{0,1},{1,0},{2,3},{3,2},{4,5},{5,4},{6,7},{7,6},{8,9},{9,8},{10,11... | collective-permute-start | bytes 442376 | tf_op jit(solution)/shard_map/ppermute | solution.py:293
  27.5 1.0 %collective-permute-done = bf16[32,9,2,128]{3,2,1,0:T(2,128)(2,1)S(1)} collective-permute-done((bf16[32,9,2,128]{3,2,1,0:T(2,128)(2,1)S(1)}, bf16[32,9,2,128]{3,2,1,0:T(2,128)(2,1)S(1)}, u32[]{:S(2)}, u32[]{:S(2)}) %collective-permute-start) | collective-permute-done | bytes 147488 | tf_op jit(solution)/shard_map/ppermute | solution.py:293
  28.5 0.5 shard_map.65
  29.0 13.4 %all_to_all.21 = f16[32,9,2,128]{3,2,1,0:T(2,128)(2,1)S(1)} all-to-all(f16[32,9,2,128]{3,2,1,0:T(2,128)(2,1)S(1)} %bitcast.18), channel_id=1, replica_groups=mesh['crop'=4,'chip'=32,'core'=2] {'chip'}, dimensions={0} | all-to-all | bytes 294912 | tf_op jit(solution)/shard_map/all_to_all | solution.py:290
  42.4 0.7 shard_map.66
  43.1 14.3 %all_to_all.22 = bf16[32,18,2,128]{3,2,1,0:T(2,128)(2,1)S(1)} all-to-all(bf16[32,18,2,128]{3,2,1,0:T(2,128)(2,1)S(1)} %bitcast.16), channel_id=1, replica_groups=mesh['crop'=4,'chip'=32,'core'=2] {'chip'}, dimensions={0} | all-to-all | bytes 589824 | tf_op jit(solution)/shard_map/all_to_all | solution.py:290
  57.4 0.4 shard_map.67
  57.9 4.1 %collective-permute-start.1 = (f16[576,128]{1,0:T(8,128)(2,1)S(1)}, f16[576,128]{1,0:T(8,128)(2,1)S(1)}, u32[]{:S(2)}, u32[]{:S(2)}) collective-permute-start(f16[576,128]{1,0:T(8,128)(2,1)S(1)} %convert_element_type.54), channel_id=1, source_target_pairs={{0,1},{1,0},{2,3},{3,2},{4,5},{5,4},{6,7},{7,6},{8,9},{9,8},{10,11... | collective-permute-start | bytes 442376 | tf_op jit(solution)/shard_map/ppermute | solution.py:293
  62.0 1.0 %collective-permute-done.1 = f16[576,128]{1,0:T(8,128)(2,1)S(1)} collective-permute-done((f16[576,128]{1,0:T(8,128)(2,1)S(1)}, f16[576,128]{1,0:T(8,128)(2,1)S(1)}, u32[]{:S(2)}, u32[]{:S(2)}) %collective-permute-start.1) | collective-permute-done | bytes 147488 | tf_op jit(solution)/shard_map/ppermute | solution.py:293
  63.1 13.4 %all_to_all.23 = f16[32,9,2,128]{3,2,1,0:T(2,128)(2,1)S(1)} all-to-all(f16[32,9,2,128]{3,2,1,0:T(2,128)(2,1)S(1)} %bitcast.21), channel_id=1, replica_groups=mesh['crop'=4,'chip'=32,'core'=2] {'chip'}, dimensions={0} | all-to-all | bytes 294912 | tf_op jit(solution)/shard_map/all_to_all | solution.py:290
  76.5 1.1 %shard_map.68 = f32[3,192,128]{2,1,0:T(8,128)} custom-call(f32[576,128]{1,0:T(8,128)S(1)} %convert.9.got, f32[128,576]{1,0:T(8,128)S(1)} %get-tuple-element.41.state, f32[128,576]{1,0:T(8,128)S(1)} %get-tuple-element.42.gate, f32[3,128,128]{2,1,0:T(8,128)S(1)} %get-tuple-element.33.gains, f32[2,128,128]{2,1,0:T(8,128)S(1)} %get-tuple-element.34.units, ...), custom_call_target="tpu_custom_call" | custom-call | tf_op jit(solution)/shard_map/pallas_call | solution.py:279
  (10 shorter events, 0.3 us)
Async XLA Ops:
  23.4 5.0 %collective-permute-start = (bf16[32,9,2,128]{3,2,1,0:T(2,128)(2,1)S(1)}, bf16[32,9,2,128]{3,2,1,0:T(2,128)(2,1)S(1)}, u32[]{:S(2)}, u32[]{:S(2)}) collective-permute-start(bf16[32,9,2,128]{3,2,1,0:T(2,128)(2,1)S(1)} %slice.4), channel_id=1, source_target_pairs={{0,1},{1,0},{2,3},{3,2},{4,5},{5,4},{6,7},{7,6},{8,9},{9,8},{10,11... | collective-permute-start | bytes 442376 | tf_op jit(solution)/shard_map/ppermute | solution.py:293
  57.9 5.1 %collective-permute-start.1 = (f16[576,128]{1,0:T(8,128)(2,1)S(1)}, f16[576,128]{1,0:T(8,128)(2,1)S(1)}, u32[]{:S(2)}, u32[]{:S(2)}) collective-permute-start(f16[576,128]{1,0:T(8,128)(2,1)S(1)} %convert_element_type.54), channel_id=1, source_target_pairs={{0,1},{1,0},{2,3},{3,2},{4,5},{5,4},{6,7},{7,6},{8,9},{9,8},{10,11... | collective-permute-start | bytes 442376 | tf_op jit(solution)/shard_map/ppermute | solution.py:293

commit v10 on v9

--- a/solution.py
+++ b/solution.py
@@ -153,9 +153,11 @@
     tri = jnp.concatenate(tri, axis=1) * spread(units[0], places)
     value = state[...] + gate[...] * mix(w_out[0], norm_rows(tri, gains[0]))
     state_next[...] = value
-    normed[...] = norm_rows(value, gains[2])
+    ready = norm_rows(value, gains[2])
+    normed[...] = ready
     each = w_proj.shape[2] // 2
-    put_edges(both, [mix(w_proj[1][:, k : k + each], normed[...]) for k in (0, each)])
+    proj = mix(w_proj[1], ready)
+    put_edges(both, (proj[:each], proj[each:]))
 
 
 def last_kernel(got, state, gate, gains, units, w_out, out, near, sems):
@@ -216,8 +218,8 @@
     return 1.02 * cols * hidden * jnp.sqrt(left * right) + 1e-20
 
 
-def outgoing_kernel(
-    got, other, normed, norm_in, w_proj, w_gate, norm_mid, out, gate, gains, units, scales
+def prepare_kernel(
+    got, normed, norm_in, w_proj, w_gate, norm_mid, left, own, gate, gains, units, scales
 ):
     parts = scales.shape[1] // OWN
     for which in range(2):
@@ -227,39 +229,58 @@
         units[which] = wide(bound * (1 / TOP))
         gains[which] = wide(norm_mid[which : which + 1, :])
     gains[2] = gain
+    for chan in range(OWN):
+        left[chan] = stack(square(take_tiles(got, 0, chan, parts)))
+        own[chan] = stack(square(take_tiles(got, 18, chan, parts)))
+    gate[...] = sigmoid(mix(w_gate[0], normed[...]))
+
+
+def outgoing_kernel(left, own, other, scales, out):
+    parts = scales.shape[1] // OWN
     first = lax.axis_index("core") == 0
     tiles = []
     for chan in range(OWN):
-        left = stack(square(take_tiles(got, 0, chan, parts)))
-        own = square(take_tiles(got, 18, chan, parts))
-        far = square(take_tiles(other, 0, chan, parts))
+        far = stack(square(take_tiles(other, 0, chan, parts)))
         right = []
-        for mine, theirs in zip(own, far):
+        for k in range(0, far.shape[0], parts):
+            mine, theirs = own[chan, k : k + parts], far[k : k + parts]
             right += [jnp.where(first, mine, theirs), jnp.where(first, theirs, mine)]
         tri = lax.dot_general(
-            left, stack(right), (((1,), (1,)), ((), ())), preferred_element_type=F32
+            left[chan],
+            jnp.concatenate(right, axis=0),
+            (((1,), (1,)), ((), ())),
+            preferred_element_type=F32,
         )
         rows = [tri[k : k + parts] for k in range(0, tri.shape[0], parts)]
         tiles.append(product_tiles(rows, scale_of(scales.at[0], chan)))
     put_tiles(out, tiles, 0)
-    gate[...] = sigmoid(mix(w_gate[0], normed[...]))
-
-
-def incoming_kernel(got, normed, w_gate, scales, out, out_other, gate):
+
+
+def half_sums(got, scales, out, core):
     parts = scales.shape[1] // OWN
-    first = lax.axis_index("core") == 0
-    kept, given = [], []
+    first = core == 0
+    tiles, sums = [], []
     for chan in range(OWN):
         left = stack(square(take_tiles(got, 0, chan, parts)))
         right = stack(square(take_tiles(got, 18, chan, parts)))
-        tri = mix(left, right)
+        turned = jnp.transpose(left)
+        rows = [turned[k : k + parts] for k in range(0, turned.shape[0], parts)]
+        rows = [jnp.where(first, a, b) for a, b in zip(rows[0::2], rows[1::2])]
+        sums.append(
+            jnp.dot(jnp.concatenate(rows, axis=0), right, preferred_element_type=F32)
+        )
+    for chan, tri in enumerate(sums):
         rows = [tri[k : k + parts] for k in range(0, tri.shape[0], parts)]
-        pairs = list(zip(rows[0::2], rows[1::2]))
-        scale = scale_of(scales.at[1], chan)
-        kept.append(product_tiles([jnp.where(first, a, b) for a, b in pairs], scale))
-        given.append(product_tiles([jnp.where(first, b, a) for a, b in pairs], scale))
-    put_tiles(out, kept, 0)
-    put_tiles(out_other, given, 0)
+        tiles.append(product_tiles(rows, scale_of(scales.at[1], chan)))
+    put_tiles(out, tiles, 0)
+
+
+def given_kernel(got, scales, out):
+    half_sums(got, scales, out, 1 - lax.axis_index("core"))
+
+
+def kept_kernel(got, scales, normed, w_gate, out, gate):
+    half_sums(got, scales, out, lax.axis_index("core"))
     gate[...] = sigmoid(mix(w_gate[1], normed[...]))
 
 
@@ -311,22 +332,25 @@
     )
     got = exchange(both.astype(BF16))
     other = swap(got[:, got.shape[1] // 2 :])
-    tri, gate, gains, units, scales = call(
-        outgoing_kernel,
-        (rows_of(got), rows_of(other), normed, norm_in, w_proj, w_gate, norm_mid),
-        [tri_t, flat_t, squares(3), squares(2), squares(2)],
-    )
+    got = rows_of(got)
+    square_t = jax.ShapeDtypeStruct((OWN, cols // CORES, cols), BF16)
+    left, own, gate, gains, units, scales = call(
+        prepare_kernel,
+        (got, normed, norm_in, w_proj, w_gate, norm_mid),
+        [square_t, square_t, flat_t, squares(3), squares(2), squares(2)],
+    )
+    (tri,) = call(outgoing_kernel, (left, own, rows_of(other), scales), [tri_t])
     got = exchange(tri.astype(jnp.float16))
     both, normed, state = call(
         middle_kernel,
         (rows_of(got), state, gate, w_proj, gains, units, w_out),
         [both_t, normed_t, flat_t],
     )
-    got = exchange(both.astype(BF16))
-    tri, given, gate = call(
-        incoming_kernel, (rows_of(got), normed, w_gate, scales), [tri_t, tri_t, flat_t]
-    )
-    tri = tri + swap(given.astype(jnp.float16)).astype(F32)
+    got = rows_of(exchange(both.astype(BF16)))
+    (given,) = call(given_kernel, (got, scales), [tri_t])
+    other = swap(given.astype(jnp.float16))
+    tri, gate = call(kept_kernel, (got, scales, normed, w_gate), [tri_t, flat_t])
+    tri = tri + other.astype(F32)
     got = exchange(tri.astype(jnp.float16))
     (out,) = call(
         last_kernel,

time: 78.6 us -> 78.5 us (level)
    pallas_call x5 -> x7, Pallas kernels: 4.38 us -> 5.01 us  [call(): pl.pallas_call(kernel, in_specs=[in_spec] * len(ins), out_specs=[out_spec...]
  transfers between devices with their start and end apart: 2 -> 2, of which waited for: 2 -> 2; matrix products, arithmetic and copies ran while one was open for 0% -> 0% of each run, Pallas kernels for 0% -> 1%
where the time goes in v10:
time: 78.5 us; the launch traced here: 77.5 us
  blocking collectives  62.6 us (80%)
  starting transfers between devices  8.13 us (10%)
  Pallas kernels  5.01 us (6%)
  waiting for transfers between devices  1.22 us (2%)
    all_to_all x4, blocking collectives, exchange(): return lax.all_to_all(sent, 'chip', 0, 0, tiled=True)  62.6 us
    ppermute x2, starting transfers between devices, swap(): return lax.ppermute(value, 'core', [(0, 1), (1, 0)])  8.13 us
    pallas_call x7, Pallas kernels, call(): pl.pallas_call(kernel, in_specs=[in_spec] * len(ins), out_specs=[out_spec...  5.01 us
  transfers between devices with their start and end apart: 2, of which 2 were waited for; matrix products, arithmetic and copies ran while one was open for 0% of the time, Pallas kernels for 1%

profile of v10, /device:TPU:1, one launch (start us, length us, event | category | flops | bytes accessed | tf_op | source)
XLA Modules:
  0.0 77.5 jit_solution(11564340983080273559)
XLA Ops:
  0.0 1.7 %shard_map.64 = (f32[1152,128]{1,0:T(8,128)S(1)}, bf16[128,576]{1,0:T(8,128)(2,1)S(1)}, f32[128,576]{1,0:T(8,128)S(1)}, f32[2,128]{1,0:T(2,128)S(1)}, bf16[2,128...) custom-call(f32[3,192,128]{2,1,0:T(8,128)} %pair.1, ...), custom_call_target="tpu_custom_call" | custom-call | tf_op jit(solution)/shard_map/pallas_call | solution.py:300
  1.7 21.6 %all_to_all.20 = bf16[32,18,2,128]{3,2,1,0:T(2,128)(2,1)S(1)} all-to-all(bf16[32,18,2,128]{3,2,1,0:T(2,128)(2,1)S(1)} %bitcast.15), channel_id=1, replica_groups=mesh['crop'=4,'chip'=32,'core'=2] {'chip'}, dimensions={0} | all-to-all | bytes 589824 | tf_op jit(solution)/shard_map/all_to_all | solution.py:311
  23.3 0.1 slice.4
  23.4 4.0 %collective-permute-start = (bf16[32,9,2,128]{3,2,1,0:T(2,128)(2,1)S(1)}, bf16[32,9,2,128]{3,2,1,0:T(2,128)(2,1)S(1)}, u32[]{:S(2)}, u32[]{:S(2)}) collective-permute-start(bf16[32,9,2,128]{3,2,1,0:T(2,128)(2,1)S(1)} %slice.4), channel_id=1, source_target_pairs={{0,1},{1,0},{2,3},{3,2},{4,5},{5,4},{6,7},{7,6},{8,9},{9,8},{10,11... | collective-permute-start | bytes 442376 | tf_op jit(solution)/shard_map/ppermute | solution.py:314
  27.5 0.4 shard_map.65
  27.9 0.6 collective-permute-done
  28.5 0.4 shard_map.66
  28.9 13.4 %all_to_all.21 = f16[32,9,2,128]{3,2,1,0:T(2,128)(2,1)S(1)} all-to-all(f16[32,9,2,128]{3,2,1,0:T(2,128)(2,1)S(1)} %bitcast.18), channel_id=1, replica_groups=mesh['crop'=4,'chip'=32,'core'=2] {'chip'}, dimensions={0} | all-to-all | bytes 294912 | tf_op jit(solution)/shard_map/all_to_all | solution.py:311
  42.3 0.7 shard_map.67
  43.0 14.3 %all_to_all.22 = bf16[32,18,2,128]{3,2,1,0:T(2,128)(2,1)S(1)} all-to-all(bf16[32,18,2,128]{3,2,1,0:T(2,128)(2,1)S(1)} %bitcast.16), channel_id=1, replica_groups=mesh['crop'=4,'chip'=32,'core'=2] {'chip'}, dimensions={0} | all-to-all | bytes 589824 | tf_op jit(solution)/shard_map/all_to_all | solution.py:311
  57.3 0.4 shard_map.69
  57.8 4.1 %collective-permute-start.1 = (f16[576,128]{1,0:T(8,128)(2,1)S(1)}, f16[576,128]{1,0:T(8,128)(2,1)S(1)}, u32[]{:S(2)}, u32[]{:S(2)}) collective-permute-start(f16[576,128]{1,0:T(8,128)(2,1)S(1)} %convert_element_type.54), channel_id=1, source_target_pairs={{0,1},{1,0},{2,3},{3,2},{4,5},{5,4},{6,7},{7,6},{8,9},{9,8},{10,11... | collective-permute-start | bytes 442376 | tf_op jit(solution)/shard_map/ppermute | solution.py:314
  61.9 0.4 shard_map.68
  62.3 0.6 collective-permute-done.1
  63.0 13.4 %all_to_all.23 = f16[32,9,2,128]{3,2,1,0:T(2,128)(2,1)S(1)} all-to-all(f16[32,9,2,128]{3,2,1,0:T(2,128)(2,1)S(1)} %bitcast.21), channel_id=1, replica_groups=mesh['crop'=4,'chip'=32,'core'=2] {'chip'}, dimensions={0} | all-to-all | bytes 294912 | tf_op jit(solution)/shard_map/all_to_all | solution.py:311
  76.4 1.1 %shard_map.70 = f32[3,192,128]{2,1,0:T(8,128)} custom-call(f32[576,128]{1,0:T(8,128)S(1)} %convert.9.got, f32[128,576]{1,0:T(8,128)S(1)} %get-tuple-element.41.state, f32[128,576]{1,0:T(8,128)S(1)} %get-tuple-element.42.gate, f32[3,128,128]{2,1,0:T(8,128)S(1)} %get-tuple-element.35.gains, f32[2,128,128]{2,1,0:T(8,128)S(1)} %get-tuple-element.36.units, ...), custom_call_target="tpu_custom_call" | custom-call | tf_op jit(solution)/shard_map/pallas_call | solution.py:300
  (10 shorter events, 0.3 us)
Async XLA Ops:
  23.4 5.0 %collective-permute-start = (bf16[32,9,2,128]{3,2,1,0:T(2,128)(2,1)S(1)}, bf16[32,9,2,128]{3,2,1,0:T(2,128)(2,1)S(1)}, u32[]{:S(2)}, u32[]{:S(2)}) collective-permute-start(bf16[32,9,2,128]{3,2,1,0:T(2,128)(2,1)S(1)} %slice.4), channel_id=1, source_target_pairs={{0,1},{1,0},{2,3},{3,2},{4,5},{5,4},{6,7},{7,6},{8,9},{9,8},{10,11... | collective-permute-start | bytes 442376 | tf_op jit(solution)/shard_map/ppermute | solution.py:314
  57.8 5.1 %collective-permute-start.1 = (f16[576,128]{1,0:T(8,128)(2,1)S(1)}, f16[576,128]{1,0:T(8,128)(2,1)S(1)}, u32[]{:S(2)}, u32[]{:S(2)}) collective-permute-start(f16[576,128]{1,0:T(8,128)(2,1)S(1)} %convert_element_type.54), channel_id=1, source_target_pairs={{0,1},{1,0},{2,3},{3,2},{4,5},{5,4},{6,7},{7,6},{8,9},{9,8},{10,11... | collective-permute-start | bytes 442376 | tf_op jit(solution)/shard_map/ppermute | solution.py:314

commit v11 on v10

--- a/solution.py
+++ b/solution.py
@@ -42,8 +42,8 @@
     return lax.dot_general(weight, value, (((0,), (0,)), ((), ())), preferred_element_type=F32)
 
 
-def sigmoid(value):
-    return 0.5 * jnp.tanh(0.5 * value) + 0.5
+def sigmoid(half):
+    return 0.5 * jnp.tanh(half) + 0.5
 
 
 def lane_tiles(value):
@@ -84,7 +84,7 @@
     hidden = proj[0].shape[0] // 2
     parts = hidden // OWN
     for side, p in enumerate(proj):
-        edge = sigmoid(p[:hidden]) * p[hidden:]
+        edge = (jnp.tanh(p[:hidden]) + 1.0) * p[hidden:]
         tiles = [lane_tiles(edge[k : k + parts]) for k in range(0, hidden, parts)]
         put_tiles(both, tiles, side * 18)
 
@@ -137,7 +137,7 @@
         )
     )
     state[...] = value
-    gain = wide(norm_in_near[0:1, :])
+    gain = wide(0.5 * norm_in_near[0:1, :])
     moves[7].wait()
     normed[...] = norm_rows(value, gain)
     proj = mix(w_proj_near[0], normed[...])
@@ -228,7 +228,7 @@
         scales[which] = wide(TOP / bound)
         units[which] = wide(bound * (1 / TOP))
         gains[which] = wide(norm_mid[which : which + 1, :])
-    gains[2] = gain
+    gains[2] = 0.5 * gain
     for chan in range(OWN):
         left[chan] = stack(square(take_tiles(got, 0, chan, parts)))
         own[chan] = stack(square(take_tiles(got, 18, chan, parts)))

time: 78.5 us -> 78.5 us (level)
  no operation moved by 1% of the time
where the time goes in v11:
time: 78.5 us; the launch traced here: 77.5 us
  blocking collectives  62.6 us (80%)
  starting transfers between devices  8.13 us (10%)
  Pallas kernels  5 us (6%)
  waiting for transfers between devices  1.22 us (2%)
    all_to_all x4, blocking collectives, exchange(): return lax.all_to_all(sent, 'chip', 0, 0, tiled=True)  62.6 us
    ppermute x2, starting transfers between devices, swap(): return lax.ppermute(value, 'core', [(0, 1), (1, 0)])  8.13 us
    pallas_call x7, Pallas kernels, call(): pl.pallas_call(kernel, in_specs=[in_spec] * len(ins), out_specs=[out_spec...  5 us
  transfers between devices with their start and end apart: 2, of which 2 were waited for; matrix products, arithmetic and copies ran while one was open for 0% of the time, Pallas kernels for 1%

profile of v11, /device:TPU:1, one launch (start us, length us, event | category | flops | bytes accessed | tf_op | source)
XLA Modules:
  0.0 77.5 jit_solution(2001075749373150138)
XLA Ops:
  0.0 1.7 %shard_map.64 = (f32[1152,128]{1,0:T(8,128)S(1)}, bf16[128,576]{1,0:T(8,128)(2,1)S(1)}, f32[128,576]{1,0:T(8,128)S(1)}, f32[2,128]{1,0:T(2,128)S(1)}, bf16[2,128...) custom-call(f32[3,192,128]{2,1,0:T(8,128)} %pair.1, ...), custom_call_target="tpu_custom_call" | custom-call | tf_op jit(solution)/shard_map/pallas_call | solution.py:300
  1.7 21.6 %all_to_all.20 = bf16[32,18,2,128]{3,2,1,0:T(2,128)(2,1)S(1)} all-to-all(bf16[32,18,2,128]{3,2,1,0:T(2,128)(2,1)S(1)} %bitcast.15), channel_id=1, replica_groups=mesh['crop'=4,'chip'=32,'core'=2] {'chip'}, dimensions={0} | all-to-all | bytes 589824 | tf_op jit(solution)/shard_map/all_to_all | solution.py:311
  23.3 0.1 slice.4
  23.4 4.0 %collective-permute-start = (bf16[32,9,2,128]{3,2,1,0:T(2,128)(2,1)S(1)}, bf16[32,9,2,128]{3,2,1,0:T(2,128)(2,1)S(1)}, u32[]{:S(2)}, u32[]{:S(2)}) collective-permute-start(bf16[32,9,2,128]{3,2,1,0:T(2,128)(2,1)S(1)} %slice.4), channel_id=1, source_target_pairs={{0,1},{1,0},{2,3},{3,2},{4,5},{5,4},{6,7},{7,6},{8,9},{9,8},{10,11... | collective-permute-start | bytes 442376 | tf_op jit(solution)/shard_map/ppermute | solution.py:314
  27.5 0.4 shard_map.65
  27.9 0.6 collective-permute-done
  28.5 0.4 shard_map.66
  28.9 13.4 %all_to_all.21 = f16[32,9,2,128]{3,2,1,0:T(2,128)(2,1)S(1)} all-to-all(f16[32,9,2,128]{3,2,1,0:T(2,128)(2,1)S(1)} %bitcast.18), channel_id=1, replica_groups=mesh['crop'=4,'chip'=32,'core'=2] {'chip'}, dimensions={0} | all-to-all | bytes 294912 | tf_op jit(solution)/shard_map/all_to_all | solution.py:311
  42.3 0.7 shard_map.67
  43.0 14.3 %all_to_all.22 = bf16[32,18,2,128]{3,2,1,0:T(2,128)(2,1)S(1)} all-to-all(bf16[32,18,2,128]{3,2,1,0:T(2,128)(2,1)S(1)} %bitcast.16), channel_id=1, replica_groups=mesh['crop'=4,'chip'=32,'core'=2] {'chip'}, dimensions={0} | all-to-all | bytes 589824 | tf_op jit(solution)/shard_map/all_to_all | solution.py:311
  57.3 0.4 shard_map.69
  57.8 4.1 %collective-permute-start.1 = (f16[576,128]{1,0:T(8,128)(2,1)S(1)}, f16[576,128]{1,0:T(8,128)(2,1)S(1)}, u32[]{:S(2)}, u32[]{:S(2)}) collective-permute-start(f16[576,128]{1,0:T(8,128)(2,1)S(1)} %convert_element_type.54), channel_id=1, source_target_pairs={{0,1},{1,0},{2,3},{3,2},{4,5},{5,4},{6,7},{7,6},{8,9},{9,8},{10,11... | collective-permute-start | bytes 442376 | tf_op jit(solution)/shard_map/ppermute | solution.py:314
  61.9 0.4 shard_map.68
  62.3 0.6 collective-permute-done.1
  63.0 13.4 %all_to_all.23 = f16[32,9,2,128]{3,2,1,0:T(2,128)(2,1)S(1)} all-to-all(f16[32,9,2,128]{3,2,1,0:T(2,128)(2,1)S(1)} %bitcast.21), channel_id=1, replica_groups=mesh['crop'=4,'chip'=32,'core'=2] {'chip'}, dimensions={0} | all-to-all | bytes 294912 | tf_op jit(solution)/shard_map/all_to_all | solution.py:311
  76.4 1.1 %shard_map.70 = f32[3,192,128]{2,1,0:T(8,128)} custom-call(f32[576,128]{1,0:T(8,128)S(1)} %convert.9.got, f32[128,576]{1,0:T(8,128)S(1)} %get-tuple-element.41.state, f32[128,576]{1,0:T(8,128)S(1)} %get-tuple-element.42.gate, f32[3,128,128]{2,1,0:T(8,128)S(1)} %get-tuple-element.35.gains, f32[2,128,128]{2,1,0:T(8,128)S(1)} %get-tuple-element.36.units, ...), custom_call_target="tpu_custom_call" | custom-call | tf_op jit(solution)/shard_map/pallas_call | solution.py:300
  (10 shorter events, 0.3 us)
Async XLA Ops:
  23.4 5.0 %collective-permute-start = (bf16[32,9,2,128]{3,2,1,0:T(2,128)(2,1)S(1)}, bf16[32,9,2,128]{3,2,1,0:T(2,128)(2,1)S(1)}, u32[]{:S(2)}, u32[]{:S(2)}) collective-permute-start(bf16[32,9,2,128]{3,2,1,0:T(2,128)(2,1)S(1)} %slice.4), channel_id=1, source_target_pairs={{0,1},{1,0},{2,3},{3,2},{4,5},{5,4},{6,7},{7,6},{8,9},{9,8},{10,11... | collective-permute-start | bytes 442376 | tf_op jit(solution)/shard_map/ppermute | solution.py:314
  57.8 5.1 %collective-permute-start.1 = (f16[576,128]{1,0:T(8,128)(2,1)S(1)}, f16[576,128]{1,0:T(8,128)(2,1)S(1)}, u32[]{:S(2)}, u32[]{:S(2)}) collective-permute-start(f16[576,128]{1,0:T(8,128)(2,1)S(1)} %convert_element_type.54), channel_id=1, source_target_pairs={{0,1},{1,0},{2,3},{3,2},{4,5},{5,4},{6,7},{7,6},{8,9},{9,8},{10,11... | collective-permute-start | bytes 442376 | tf_op jit(solution)/shard_map/ppermute | solution.py:314

commit v12 on v10

--- a/solution.py
+++ b/solution.py
@@ -139,8 +139,9 @@
     state[...] = value
     gain = wide(norm_in_near[0:1, :])
     moves[7].wait()
-    normed[...] = norm_rows(value, gain)
-    proj = mix(w_proj_near[0], normed[...])
+    ready = norm_rows(value, gain)
+    normed[...] = ready
+    proj = mix(w_proj_near[0], ready)
     put_edges(both, (proj[: 2 * chans], proj[2 * chans :]))
     for move in moves[8:]:
         move.wait()

time: 78.5 us -> 78.5 us (level)
  no operation moved by 1% of the time
where the time goes in v12:
time: 78.5 us; the launch traced here: 77.5 us
  blocking collectives  62.6 us (80%)
  starting transfers between devices  8.13 us (10%)
  Pallas kernels  5 us (6%)
  waiting for transfers between devices  1.22 us (2%)
    all_to_all x4, blocking collectives, exchange(): return lax.all_to_all(sent, 'chip', 0, 0, tiled=True)  62.6 us
    ppermute x2, starting transfers between devices, swap(): return lax.ppermute(value, 'core', [(0, 1), (1, 0)])  8.13 us
    pallas_call x7, Pallas kernels, call(): pl.pallas_call(kernel, in_specs=[in_spec] * len(ins), out_specs=[out_spec...  5 us
  transfers between devices with their start and end apart: 2, of which 2 were waited for; matrix products, arithmetic and copies ran while one was open for 0% of the time, Pallas kernels for 1%

profile of v12, /device:TPU:1, one launch (start us, length us, event | category | flops | bytes accessed | tf_op | source)
XLA Modules:
  0.0 77.5 jit_solution(543829017777296172)
XLA Ops:
  0.0 1.7 %shard_map.64 = (f32[1152,128]{1,0:T(8,128)S(1)}, bf16[128,576]{1,0:T(8,128)(2,1)S(1)}, f32[128,576]{1,0:T(8,128)S(1)}, f32[2,128]{1,0:T(2,128)S(1)}, bf16[2,128...) custom-call(f32[3,192,128]{2,1,0:T(8,128)} %pair.1, ...), custom_call_target="tpu_custom_call" | custom-call | tf_op jit(solution)/shard_map/pallas_call | solution.py:301
  1.7 21.6 %all_to_all.20 = bf16[32,18,2,128]{3,2,1,0:T(2,128)(2,1)S(1)} all-to-all(bf16[32,18,2,128]{3,2,1,0:T(2,128)(2,1)S(1)} %bitcast.15), channel_id=1, replica_groups=mesh['crop'=4,'chip'=32,'core'=2] {'chip'}, dimensions={0} | all-to-all | bytes 589824 | tf_op jit(solution)/shard_map/all_to_all | solution.py:312
  23.3 0.1 slice.4
  23.4 4.0 %collective-permute-start = (bf16[32,9,2,128]{3,2,1,0:T(2,128)(2,1)S(1)}, bf16[32,9,2,128]{3,2,1,0:T(2,128)(2,1)S(1)}, u32[]{:S(2)}, u32[]{:S(2)}) collective-permute-start(bf16[32,9,2,128]{3,2,1,0:T(2,128)(2,1)S(1)} %slice.4), channel_id=1, source_target_pairs={{0,1},{1,0},{2,3},{3,2},{4,5},{5,4},{6,7},{7,6},{8,9},{9,8},{10,11... | collective-permute-start | bytes 442376 | tf_op jit(solution)/shard_map/ppermute | solution.py:315
  27.5 0.4 shard_map.65
  27.9 0.6 collective-permute-done
  28.5 0.4 shard_map.66
  28.9 13.4 %all_to_all.21 = f16[32,9,2,128]{3,2,1,0:T(2,128)(2,1)S(1)} all-to-all(f16[32,9,2,128]{3,2,1,0:T(2,128)(2,1)S(1)} %bitcast.18), channel_id=1, replica_groups=mesh['crop'=4,'chip'=32,'core'=2] {'chip'}, dimensions={0} | all-to-all | bytes 294912 | tf_op jit(solution)/shard_map/all_to_all | solution.py:312
  42.3 0.7 shard_map.67
  43.0 14.3 %all_to_all.22 = bf16[32,18,2,128]{3,2,1,0:T(2,128)(2,1)S(1)} all-to-all(bf16[32,18,2,128]{3,2,1,0:T(2,128)(2,1)S(1)} %bitcast.16), channel_id=1, replica_groups=mesh['crop'=4,'chip'=32,'core'=2] {'chip'}, dimensions={0} | all-to-all | bytes 589824 | tf_op jit(solution)/shard_map/all_to_all | solution.py:312
  57.3 0.4 shard_map.69
  57.8 4.1 %collective-permute-start.1 = (f16[576,128]{1,0:T(8,128)(2,1)S(1)}, f16[576,128]{1,0:T(8,128)(2,1)S(1)}, u32[]{:S(2)}, u32[]{:S(2)}) collective-permute-start(f16[576,128]{1,0:T(8,128)(2,1)S(1)} %convert_element_type.54), channel_id=1, source_target_pairs={{0,1},{1,0},{2,3},{3,2},{4,5},{5,4},{6,7},{7,6},{8,9},{9,8},{10,11... | collective-permute-start | bytes 442376 | tf_op jit(solution)/shard_map/ppermute | solution.py:315
  61.9 0.4 shard_map.68
  62.3 0.6 collective-permute-done.1
  63.0 13.4 %all_to_all.23 = f16[32,9,2,128]{3,2,1,0:T(2,128)(2,1)S(1)} all-to-all(f16[32,9,2,128]{3,2,1,0:T(2,128)(2,1)S(1)} %bitcast.21), channel_id=1, replica_groups=mesh['crop'=4,'chip'=32,'core'=2] {'chip'}, dimensions={0} | all-to-all | bytes 294912 | tf_op jit(solution)/shard_map/all_to_all | solution.py:312
  76.4 1.1 %shard_map.70 = f32[3,192,128]{2,1,0:T(8,128)} custom-call(f32[576,128]{1,0:T(8,128)S(1)} %convert.9.got, f32[128,576]{1,0:T(8,128)S(1)} %get-tuple-element.41.state, f32[128,576]{1,0:T(8,128)S(1)} %get-tuple-element.42.gate, f32[3,128,128]{2,1,0:T(8,128)S(1)} %get-tuple-element.35.gains, f32[2,128,128]{2,1,0:T(8,128)S(1)} %get-tuple-element.36.units, ...), custom_call_target="tpu_custom_call" | custom-call | tf_op jit(solution)/shard_map/pallas_call | solution.py:301
  (10 shorter events, 0.3 us)
Async XLA Ops:
  23.4 5.0 %collective-permute-start = (bf16[32,9,2,128]{3,2,1,0:T(2,128)(2,1)S(1)}, bf16[32,9,2,128]{3,2,1,0:T(2,128)(2,1)S(1)}, u32[]{:S(2)}, u32[]{:S(2)}) collective-permute-start(bf16[32,9,2,128]{3,2,1,0:T(2,128)(2,1)S(1)} %slice.4), channel_id=1, source_target_pairs={{0,1},{1,0},{2,3},{3,2},{4,5},{5,4},{6,7},{7,6},{8,9},{9,8},{10,11... | collective-permute-start | bytes 442376 | tf_op jit(solution)/shard_map/ppermute | solution.py:315
  57.8 5.1 %collective-permute-start.1 = (f16[576,128]{1,0:T(8,128)(2,1)S(1)}, f16[576,128]{1,0:T(8,128)(2,1)S(1)}, u32[]{:S(2)}, u32[]{:S(2)}) collective-permute-start(f16[576,128]{1,0:T(8,128)(2,1)S(1)} %convert_element_type.54), channel_id=1, source_target_pairs={{0,1},{1,0},{2,3},{3,2},{4,5},{5,4},{6,7},{7,6},{8,9},{9,8},{10,11... | collective-permute-start | bytes 442376 | tf_op jit(solution)/shard_map/ppermute | solution.py:315

commit v13 on v11

--- a/solution.py
+++ b/solution.py
@@ -139,8 +139,9 @@
     state[...] = value
     gain = wide(0.5 * norm_in_near[0:1, :])
     moves[7].wait()
-    normed[...] = norm_rows(value, gain)
-    proj = mix(w_proj_near[0], normed[...])
+    ready = norm_rows(value, gain)
+    normed[...] = ready
+    proj = mix(w_proj_near[0], ready)
     put_edges(both, (proj[: 2 * chans], proj[2 * chans :]))
     for move in moves[8:]:
         move.wait()

time: 78.5 us -> 78.5 us (level)
  no operation moved by 1% of the time
where the time goes in v13:
time: 78.5 us; the launch traced here: 77.5 us
  blocking collectives  62.6 us (80%)
  starting transfers between devices  8.13 us (10%)
  Pallas kernels  5 us (6%)
  waiting for transfers between devices  1.22 us (2%)
    all_to_all x4, blocking collectives, exchange(): return lax.all_to_all(sent, 'chip', 0, 0, tiled=True)  62.6 us
    ppermute x2, starting transfers between devices, swap(): return lax.ppermute(value, 'core', [(0, 1), (1, 0)])  8.13 us
    pallas_call x7, Pallas kernels, call(): pl.pallas_call(kernel, in_specs=[in_spec] * len(ins), out_specs=[out_spec...  5 us
  transfers between devices with their start and end apart: 2, of which 2 were waited for; matrix products, arithmetic and copies ran while one was open for 0% of the time, Pallas kernels for 1%

profile of v13, /device:TPU:1, one launch (start us, length us, event | category | flops | bytes accessed | tf_op | source)
XLA Modules:
  0.0 77.5 jit_solution(3127733106418792664)
XLA Ops:
  0.0 1.7 %shard_map.64 = (f32[1152,128]{1,0:T(8,128)S(1)}, bf16[128,576]{1,0:T(8,128)(2,1)S(1)}, f32[128,576]{1,0:T(8,128)S(1)}, f32[2,128]{1,0:T(2,128)S(1)}, bf16[2,128...) custom-call(f32[3,192,128]{2,1,0:T(8,128)} %pair.1, ...), custom_call_target="tpu_custom_call" | custom-call | tf_op jit(solution)/shard_map/pallas_call | solution.py:301
  1.7 21.6 %all_to_all.20 = bf16[32,18,2,128]{3,2,1,0:T(2,128)(2,1)S(1)} all-to-all(bf16[32,18,2,128]{3,2,1,0:T(2,128)(2,1)S(1)} %bitcast.15), channel_id=1, replica_groups=mesh['crop'=4,'chip'=32,'core'=2] {'chip'}, dimensions={0} | all-to-all | bytes 589824 | tf_op jit(solution)/shard_map/all_to_all | solution.py:312
  23.3 0.1 slice.4
  23.4 4.0 %collective-permute-start = (bf16[32,9,2,128]{3,2,1,0:T(2,128)(2,1)S(1)}, bf16[32,9,2,128]{3,2,1,0:T(2,128)(2,1)S(1)}, u32[]{:S(2)}, u32[]{:S(2)}) collective-permute-start(bf16[32,9,2,128]{3,2,1,0:T(2,128)(2,1)S(1)} %slice.4), channel_id=1, source_target_pairs={{0,1},{1,0},{2,3},{3,2},{4,5},{5,4},{6,7},{7,6},{8,9},{9,8},{10,11... | collective-permute-start | bytes 442376 | tf_op jit(solution)/shard_map/ppermute | solution.py:315
  27.5 0.4 shard_map.65
  27.9 0.6 collective-permute-done
  28.5 0.4 shard_map.66
  28.9 13.4 %all_to_all.21 = f16[32,9,2,128]{3,2,1,0:T(2,128)(2,1)S(1)} all-to-all(f16[32,9,2,128]{3,2,1,0:T(2,128)(2,1)S(1)} %bitcast.18), channel_id=1, replica_groups=mesh['crop'=4,'chip'=32,'core'=2] {'chip'}, dimensions={0} | all-to-all | bytes 294912 | tf_op jit(solution)/shard_map/all_to_all | solution.py:312
  42.3 0.7 shard_map.67
  43.0 14.3 %all_to_all.22 = bf16[32,18,2,128]{3,2,1,0:T(2,128)(2,1)S(1)} all-to-all(bf16[32,18,2,128]{3,2,1,0:T(2,128)(2,1)S(1)} %bitcast.16), channel_id=1, replica_groups=mesh['crop'=4,'chip'=32,'core'=2] {'chip'}, dimensions={0} | all-to-all | bytes 589824 | tf_op jit(solution)/shard_map/all_to_all | solution.py:312
  57.3 0.4 shard_map.69
  57.8 4.1 %collective-permute-start.1 = (f16[576,128]{1,0:T(8,128)(2,1)S(1)}, f16[576,128]{1,0:T(8,128)(2,1)S(1)}, u32[]{:S(2)}, u32[]{:S(2)}) collective-permute-start(f16[576,128]{1,0:T(8,128)(2,1)S(1)} %convert_element_type.54), channel_id=1, source_target_pairs={{0,1},{1,0},{2,3},{3,2},{4,5},{5,4},{6,7},{7,6},{8,9},{9,8},{10,11... | collective-permute-start | bytes 442376 | tf_op jit(solution)/shard_map/ppermute | solution.py:315
  61.9 0.4 shard_map.68
  62.3 0.6 collective-permute-done.1
  63.0 13.4 %all_to_all.23 = f16[32,9,2,128]{3,2,1,0:T(2,128)(2,1)S(1)} all-to-all(f16[32,9,2,128]{3,2,1,0:T(2,128)(2,1)S(1)} %bitcast.21), channel_id=1, replica_groups=mesh['crop'=4,'chip'=32,'core'=2] {'chip'}, dimensions={0} | all-to-all | bytes 294912 | tf_op jit(solution)/shard_map/all_to_all | solution.py:312
  76.4 1.1 %shard_map.70 = f32[3,192,128]{2,1,0:T(8,128)} custom-call(f32[576,128]{1,0:T(8,128)S(1)} %convert.9.got, f32[128,576]{1,0:T(8,128)S(1)} %get-tuple-element.41.state, f32[128,576]{1,0:T(8,128)S(1)} %get-tuple-element.42.gate, f32[3,128,128]{2,1,0:T(8,128)S(1)} %get-tuple-element.35.gains, f32[2,128,128]{2,1,0:T(8,128)S(1)} %get-tuple-element.36.units, ...), custom_call_target="tpu_custom_call" | custom-call | tf_op jit(solution)/shard_map/pallas_call | solution.py:301
  (10 shorter events, 0.3 us)
Async XLA Ops:
  23.4 5.0 %collective-permute-start = (bf16[32,9,2,128]{3,2,1,0:T(2,128)(2,1)S(1)}, bf16[32,9,2,128]{3,2,1,0:T(2,128)(2,1)S(1)}, u32[]{:S(2)}, u32[]{:S(2)}) collective-permute-start(bf16[32,9,2,128]{3,2,1,0:T(2,128)(2,1)S(1)} %slice.4), channel_id=1, source_target_pairs={{0,1},{1,0},{2,3},{3,2},{4,5},{5,4},{6,7},{7,6},{8,9},{9,8},{10,11... | collective-permute-start | bytes 442376 | tf_op jit(solution)/shard_map/ppermute | solution.py:315
  57.8 5.1 %collective-permute-start.1 = (f16[576,128]{1,0:T(8,128)(2,1)S(1)}, f16[576,128]{1,0:T(8,128)(2,1)S(1)}, u32[]{:S(2)}, u32[]{:S(2)}) collective-permute-start(f16[576,128]{1,0:T(8,128)(2,1)S(1)} %convert_element_type.54), channel_id=1, source_target_pairs={{0,1},{1,0},{2,3},{3,2},{4,5},{5,4},{6,7},{7,6},{8,9},{9,8},{10,11... | collective-permute-start | bytes 442376 | tf_op jit(solution)/shard_map/ppermute | solution.py:315
